TPU v7x, 128 devices: a whole 4x4x4 slice. The times are simulated.
128 devices in a mesh: tile: 32 (over y_lo, z, x), slab: 4 (over y_hi, core).
Axes of the slice: x: 4, y: 4 (y_hi: 2, y_lo: 2; y = y_hi * 2 + y_lo), z: 4, core: 2. Of those that a mesh axis runs over, the one named last changes fastest.
Arguments:
- pixels: bfloat16 [4, 128, 128, 384], P('slab', 'tile'), may hold values from -12 to 12
- tissue: int32 [4, 128, 1024], P('slab', 'tile'), may hold values from 0 to 1, as said below
- neighbours: int32 [4, 128, 8], P('slab', 'tile'), may hold values from -1 to 127, as said below
- upstream: bfloat16 [4, 128, 32, 3072], P('slab', 'tile'), may hold values from -6 to 6
- stem_weight: bfloat16 [48, 96], replicated, may hold values from -0.875 to 0.875
- stem_gain: float32 [96], replicated, may hold values from 0.5 to 1.5
- dw_weight: float32 [49, 96], replicated, may hold values from -1.8 to 1.8
- norm_gain: float32 [96], replicated, may hold values from 0.5 to 1.5
- up_weight: bfloat16 [96, 384], replicated, may hold values from -0.625 to 0.625
- down_weight: bfloat16 [384, 96], replicated, may hold values from -0.3125 to 0.3125
- layer_scale: float32 [96], replicated, may hold values from 0.2 to 1
Outputs:
- features: bfloat16 [4, 128, 32, 3072], P('slab', 'tile')
- grad_dw: float32 [49, 96], replicated
- grad_gain: float32 [96], replicated
- grad_up: float32 [96, 384], replicated
- grad_down: float32 [384, 96], replicated
- grad_scale: float32 [96], replicated
Inputs may be any that keep to these rules, and one draw needn't show every extreme that they name: `neighbours`: for each tile slot, the slot (numbered within its region, device by device along tile) of the tissue tile beside it to the north, south, west, east, north-west, north-east, south-west and south-east, or -1 where there is none; -1 throughout in slots that hold no tile; the relation is symmetric. A region's tiles are numbered down the columns of a band 4 tiles high (the first tile may stand at any row of its band) and the devices of the region take them in order, each 1 to 4 consecutive tiles in its first slots; some device holds 4. So a tile beside a tile lies at most 5 devices away along tile, and in every region some lies exactly that far. 1 on cells that lie on tissue; all zero in slots that hold no tile.
All inputs are finite; a program needn't handle non-finite values.
Results may differ from a plain program's by a relative error of at most 0.0083.
Values may be sent and summed in bfloat16 or wider, within the bound.
A program may use at most 128 MiB of HBM per device.

v0:
```python
import functools

import jax
import jax.numpy as jnp
from jax import lax
from jax.experimental import pallas as pl
from jax.experimental.pallas import tpu as pltpu
from jax.sharding import PartitionSpec as P

MESH = pl.DeviceIdType.MESH
C = 96
HID = 384
PATCH = 4
KS = 7
SIDE = 32
RIM = 3
REACH = 5
SLOTS = 4
LANES = SLOTS * SIDE
PADW = SIDE + 2 * RIM
GROUP = 16
GROUPS = C // GROUP
BLOCK = 8
BLOCKS = SIDE // BLOCK
TAPW = (BLOCK + RIM * 2) * GROUP
BAND = KS * TAPW
EPS = 1e-06
CHUNKS = 16
MAIN = 48
CHUNK_ROWS = MAIN + 8

BF16 = jnp.bfloat16
F32 = jnp.float32


def iota(shape, dim):
    return lax.broadcasted_iota(jnp.int32, shape, dim)


def onehot(mask):
    return jnp.where(mask, 1.0, 0.0).astype(BF16)


def mm(a, b):
    return lax.dot_general(a, b, (((1,), (0,)), ((), ())), preferred_element_type=F32)


def mm_nt(a, b):
    return lax.dot_general(a, b, (((1,), (1,)), ((), ())), preferred_element_type=F32)


def column(row, lanes):
    return jnp.transpose(jnp.broadcast_to(row, (lanes, row.shape[1])))


def stem_kernel(tiles, pix_ref, w_ref, gain_ref, ct_ref, recv_ref, strip_ref, send_sem, recv_sem):
    me = lax.axis_index("tile")
    barrier = pltpu.get_barrier_semaphore()
    for d in range(1, REACH + 1):
        for sign in (-1, 1):
            peer = lax.rem(me + sign * d + tiles, tiles)
            pl.semaphore_signal(barrier, inc=1, device_id={"tile": peer}, device_id_type=MESH)

    pix = pix_ref[...].reshape(SLOTS * SIDE * PATCH, SIDE * PATCH * 3)
    rows = SLOTS * SIDE * PATCH
    k_at, n_at = iota((rows, rows), 0), iota((rows, rows), 1)
    pick = onehot(k_at == PATCH * (n_at % LANES) + n_at // LANES)
    pix_t = mm(jnp.transpose(pix), pick).astype(BF16)

    q = PATCH * 3
    wt = jnp.transpose(w_ref[...])
    k_at, n_at = iota((PATCH * q, PATCH * 4 * q), 0), iota((PATCH * q, PATCH * 4 * q), 1)
    spread = onehot((k_at // q == n_at // (4 * q)) & (k_at % q == n_at % q))
    wide = mm(wt, spread)
    wide = jnp.concatenate([wide] * 4, axis=0)
    r_at, n_at = iota(wide.shape, 0), iota(wide.shape, 1)
    block_w = jnp.where(r_at // C == (n_at % (4 * q)) // q, wide, 0.0).astype(BF16)

    gain = column(gain_ref[...], LANES)
    eight = SIDE // 4
    operand = jnp.concatenate(
        [
            jnp.concatenate(
                [pix_t[4 * q * g : 4 * q * (g + 1), LANES * pr : LANES * (pr + 1)] for pr in range(PATCH)],
                axis=0,
            )
            for g in range(eight)
        ],
        axis=1,
    )
    raw = mm(block_w, operand)
    for v in range(4):
        part = raw[C * v : C * (v + 1)]
        mean = jnp.sum(part, axis=0, keepdims=True) * (1.0 / C)
        part = part - mean
        inverse = lax.rsqrt(jnp.sum(part * part, axis=0, keepdims=True) * (1.0 / C) + EPS)
        part = part * inverse
        for g in range(eight):
            ct_ref[4 * g + v] = (part[:, LANES * g : LANES * (g + 1)] * gain).astype(BF16)

    k_at, n_at = iota((LANES, 6 * LANES), 0), iota((LANES, 6 * LANES), 1)
    kind = n_at // LANES
    row_at = jnp.where(kind < RIM, kind, SIDE - 2 * RIM + kind)
    base = onehot((k_at // SIDE == n_at % SLOTS) & (k_at % SIDE == row_at))
    col_of = (n_at % LANES) // SLOTS
    packed = jnp.zeros((C, 6 * LANES), F32)
    for w in range(0, SIDE, 8):
        left = jnp.concatenate([ct_ref[w + i] for i in range(8)], axis=1)
        right = jnp.concatenate(
            [jnp.where(col_of == w + i, base, jnp.zeros_like(base)) for i in range(8)], axis=0
        )
        packed = packed + mm(left, right)
    for i in range(6):
        strip_ref[i] = packed[:, LANES * i : LANES * (i + 1)].astype(BF16)

    pl.semaphore_wait(barrier, 2 * REACH)
    copies = []
    for d in range(1, REACH + 1):
        back = lax.rem(me - d + tiles, tiles)
        ahead = lax.rem(me + d, tiles)
        if d == 1:
            copies.append((strip_ref.at[pl.ds(0, RIM)], 10, back))
            copies.append((strip_ref.at[pl.ds(RIM, RIM)], 11, ahead))
        copies.append((ct_ref.at[pl.ds(0, RIM)], d - 1, back))
        copies.append((ct_ref.at[pl.ds(SIDE - RIM, RIM)], REACH + d - 1, ahead))
    started = []
    for source, at, peer in copies:
        copy = pltpu.make_async_remote_copy(
            src_ref=source,
            dst_ref=recv_ref.at[at],
            send_sem=send_sem.at[at],
            recv_sem=recv_sem.at[at],
            device_id={"tile": peer},
            device_id_type=MESH,
        )
        copy.start()
        started.append(copy)
    for copy in started:
        copy.wait()


def gelu_parts(hidden):
    normal_cdf = 0.5 * (1.0 + lax.erf(hidden * 0.7071067811865476))
    density = jnp.exp(-0.5 * hidden * hidden) * 0.3989422804014327
    return (hidden * normal_cdf, normal_cdf + hidden * density)


def block_kernel(
    loss_factor,
    nb_ref,
    ct_ref,
    recv_ref,
    up_stream_ref,
    tissue_ref,
    dw_ref,
    gain_ref,
    scale_ref,
    up_ref,
    down_ref,
    feat_ref,
    sums_ref,
    pt_ref,
    ht_ref,
    side_ref,
    mixed_ref,
    gm_ref,
    ut_ref,
    ft_ref,
    gd_ref,
    gu_ref,
    gg_ref,
    gs_ref,
):
    me = lax.axis_index("tile")
    lane = iota((1, LANES), 1)
    slot_of, row_of = lane // SIDE, lane % SIDE

    def per_tile(direction, rule):
        out = []
        for t in range(SLOTS):
            n = nb_ref[t, direction]
            out.append(jnp.where(n >= 0, rule(jnp.maximum(n, 0)), -1))
        return out

    def spread(values, shift):
        result = jnp.full((1, LANES), -1, jnp.int32)
        for t in range(SLOTS):
            result = jnp.where(slot_of == (t + shift) % SLOTS, values[t], result)
        return result

    def add_row(index, row):
        return jnp.where(index >= 0, index + row, -1)

    top = row_of >= SIDE - RIM
    bottom = row_of < RIM

    for east in (0, 1):
        def rule(n, east=east):
            away = n // SLOTS - me
            away = away if east else -away
            return away * LANES + (n % SLOTS) * SIDE

        straight = spread(per_tile(2 + east, rule), 0)
        above = spread(per_tile(4 + east, rule), -1)
        below = spread(per_tile(6 + east, rule), 1)
        halo = jnp.where(top, above, jnp.where(bottom, below, -1))
        index = jnp.concatenate([add_row(straight, row_of), add_row(halo, row_of)], axis=1)
        select = onehot(iota(((REACH + 1) * LANES, 2 * LANES), 0) == index)
        first = 0 if east else SIDE - RIM
        base = 0 if east else REACH
        for i in range(RIM):
            source = jnp.concatenate(
                [ct_ref[first + i]] + [recv_ref[base + d, i] for d in range(REACH)], axis=1
            )
            side_ref[east * RIM + i] = mm(source, select).astype(BF16)

    def own_rule(n):
        return jnp.where(n // SLOTS == me, (n % SLOTS) * SIDE, -1)

    def other_rule(n):
        return jnp.where(n // SLOTS == me, -1, n % SLOTS)

    own_above = spread(per_tile(0, own_rule), -1)
    own_below = spread(per_tile(1, own_rule), 1)
    own = add_row(jnp.where(top, own_above, jnp.where(bottom, own_below, -1)), row_of)
    select_own = onehot(iota((LANES, LANES), 0) == own)
    far_above = spread(per_tile(0, other_rule), -1)
    far_below = spread(per_tile(1, other_rule), 1)
    far = jnp.where(
        top,
        jnp.where(far_above >= 0, (row_of - (SIDE - RIM)) * SLOTS + far_above, -1),
        jnp.where(bottom & (far_below >= 0), (RIM + row_of) * SLOTS + far_below, -1),
    )
    k_at = iota((2 * RIM * LANES, LANES), 0)
    far_base = onehot((k_at // LANES) * SLOTS + k_at % SLOTS == far)
    col_of = (k_at % LANES) // SLOTS
    strips = jnp.concatenate(
        [recv_ref[11, i] for i in range(RIM)] + [recv_ref[10, i] for i in range(RIM)], axis=1
    )
    for w in range(0, SIDE, 4):
        select_far = jnp.concatenate(
            [jnp.where(col_of == w + i, far_base, jnp.zeros_like(far_base)) for i in range(4)], axis=1
        )
        got = mm(strips, select_far)
        for i in range(4):
            near = mm(ct_ref[w + i], select_own)
            ht_ref[w + i] = (near + got[:, LANES * i : LANES * (i + 1)]).astype(BF16)

    def fill(at, centre, halo):
        for a in range(KS):
            s = a - RIM
            if s > 0:
                value = pltpu.roll(jnp.where(row_of < s, halo, centre), LANES - s, 1)
            elif s < 0:
                value = pltpu.roll(jnp.where(row_of >= SIDE + s, halo, centre), -s, 1)
            else:
                value = centre
            pt_ref[a, at] = value

    for i in range(RIM):
        for east in (0, 1):
            sides = side_ref[east * RIM + i]
            fill(east * (RIM + SIDE) + i, sides[:, :LANES], sides[:, LANES:])

    def fill_step(w, carry):
        fill(RIM + w, ct_ref[w], ht_ref[w])
        return carry

    lax.fori_loop(0, SIDE, fill_step, 0)

    for w in range(0, SIDE, 4):
        part = jnp.transpose(up_stream_ref[:, C * w : C * (w + 4)])
        for i in range(4):
            ut_ref[w + i] = part[C * i : C * (i + 1)]

    def window(g):
        return jnp.concatenate(
            [
                jnp.concatenate(
                    [
                        pt_ref[a, BLOCK * j : BLOCK * j + TAPW // GROUP, GROUP * g : GROUP * (g + 1)].reshape(
                            TAPW, LANES
                        )
                        for a in range(KS)
                    ],
                    axis=0,
                )
                for j in range(BLOCKS)
            ],
            axis=1,
        )

    r_at, n_at = iota((GROUP, BAND), 0), iota((GROUP, BAND), 1)
    diagonal = r_at == n_at % GROUP
    for g in range(GROUPS):
        first = jnp.where(diagonal, dw_ref[pl.ds(g, 1), :], 0.0)
        band = jnp.concatenate(
            [first] + [pltpu.roll(first, GROUP * w, 1) for w in range(1, BLOCK)], axis=0
        ).astype(BF16)
        out = mm(band, window(g))
        for w in range(BLOCK):
            mixed_ref[w, GROUP * g : GROUP * (g + 1), :] = out[GROUP * w : GROUP * (w + 1)]

    gain = column(gain_ref[...], LANES)
    scale = column(scale_ref[...], LANES)
    gain = jnp.concatenate([gain] * BLOCKS, axis=1)
    scale = jnp.concatenate([scale] * BLOCKS, axis=1)
    up_w = up_ref[...]
    down_w = down_ref[...]
    up_t = jnp.transpose(up_w)
    down_t = jnp.transpose(down_w)
    gd_ref[...] = jnp.zeros_like(gd_ref)
    gu_ref[...] = jnp.zeros_like(gu_ref)
    gg_ref[...] = jnp.zeros_like(gg_ref)
    gs_ref[...] = jnp.zeros_like(gs_ref)

    def gather(ref, w, offset=0):
        return jnp.concatenate([ref[offset + BLOCK * j + w] for j in range(BLOCKS)], axis=1)

    def fold(values):
        total = values[:, :LANES]
        for j in range(1, BLOCKS):
            total = total + values[:, LANES * j : LANES * (j + 1)]
        return total

    def step(w, carry):
        mixed = mixed_ref[w]
        mean = jnp.sum(mixed, axis=0, keepdims=True) * (1.0 / C)
        centered = mixed - mean
        inverse = lax.rsqrt(jnp.sum(centered * centered, axis=0, keepdims=True) * (1.0 / C) + EPS)
        normed = centered * inverse
        lowered = (normed * gain).astype(BF16)
        hidden = mm(up_t, lowered)
        active, steepness = gelu_parts(hidden)
        active = active.astype(BF16)
        branch = mm(down_t, active)
        tissue = gather(tissue_ref, w)
        summed = gather(ct_ref, w).astype(F32) + scale * branch
        features = (summed * tissue).astype(BF16)
        grad_out = gather(ut_ref, w).astype(F32) * (tissue * loss_factor)
        gs_ref[...] += fold(grad_out * branch)
        grad_branch = (grad_out * scale).astype(BF16)
        gd_ref[...] += mm_nt(active, grad_branch)
        grad_active = mm(down_w, grad_branch)
        grad_hidden = (grad_active * steepness).astype(BF16)
        gu_ref[...] += mm_nt(grad_hidden, lowered)
        grad_lowered = mm(up_w, grad_hidden)
        gg_ref[...] += fold(grad_lowered * normed)
        scaled = grad_lowered * gain
        mean_one = jnp.sum(scaled, axis=0, keepdims=True) * (1.0 / C)
        mean_two = jnp.sum(scaled * normed, axis=0, keepdims=True) * (1.0 / C)
        gm_ref[w] = (inverse * (scaled - mean_one - normed * mean_two)).astype(BF16)
        for j in range(BLOCKS):
            ft_ref[BLOCK * j + w] = features[:, LANES * j : LANES * (j + 1)]
        return carry

    lax.fori_loop(0, BLOCK, step, 0)

    for w in range(0, SIDE, 4):
        part = jnp.concatenate([ft_ref[w + i] for i in range(4)], axis=0)
        feat_ref[:, C * w : C * (w + 4)] = jnp.transpose(part)

    low = []
    for g in range(GROUPS):
        left = jnp.concatenate([gm_ref[w, GROUP * g : GROUP * (g + 1), :] for w in range(BLOCK)], axis=0)
        full = mm_nt(left, window(g))
        total = None
        for w in range(BLOCK):
            part = jnp.where(diagonal, full[GROUP * w : GROUP * (w + 1)], 0.0)
            part = part[:8] + part[8:]
            if w:
                part = pltpu.roll(part, BAND - GROUP * w, 1)
            total = part if total is None else total + part
        total = jnp.sum(total, axis=0, keepdims=True)
        low.append(
            jnp.concatenate([total[:, TAPW * a : TAPW * a + KS * GROUP] for a in range(KS)], axis=1)
        )
    width = CHUNKS * 128
    filler = jnp.zeros((1, width - KS * KS * GROUP), F32)
    low = [jnp.concatenate([row, filler], axis=1) for row in low]
    for ref in (gg_ref, gs_ref):
        row = jnp.sum(jnp.transpose(ref[...]), axis=0, keepdims=True)
        low.append(jnp.concatenate([row, jnp.zeros((1, width - C), F32)], axis=1))
    low = jnp.concatenate(low, axis=0)
    padding = jnp.zeros((MAIN, 128 - C), F32)
    for i in range(CHUNKS):
        ref, at = (gd_ref, i) if i < 8 else (gu_ref, i - 8)
        rows = ref[MAIN * at : MAIN * (at + 1), :]
        sums_ref[i, :MAIN, :] = jnp.concatenate([rows, padding], axis=1)
        sums_ref[i, MAIN:, :] = low[:, 128 * i : 128 * (i + 1)]


def reduce_kernel(x_ref, gd_ref, gu_ref, low_ref, first, second, part, res, s1, r1, s2, r2, s3, r3):
    tile = lax.axis_index("tile")
    slab = lax.axis_index("slab")
    me_a = tile % 4 + 4 * slab
    me_b = tile // 4

    def peer_a(k):
        i = lax.rem(me_a + k, CHUNKS)
        return i, {"tile": me_b * 4 + i % 4, "slab": i // 4}

    def peer_b(k):
        j = lax.rem(me_b + k, 8)
        return j, {"tile": j * 4 + tile % 4, "slab": slab}

    barrier = pltpu.get_barrier_semaphore()
    for k in range(1, CHUNKS):
        pl.semaphore_signal(barrier, inc=1, device_id=peer_a(k)[1], device_id_type=MESH)
    for k in range(1, 8):
        pl.semaphore_signal(barrier, inc=1, device_id=peer_b(k)[1], device_id_type=MESH)
    pl.semaphore_wait(barrier, CHUNKS - 1 + 7)

    def send(source, target, send_sem, recv_sem, device):
        copy = pltpu.make_async_remote_copy(
            src_ref=source,
            dst_ref=target,
            send_sem=send_sem,
            recv_sem=recv_sem,
            device_id=device,
            device_id_type=MESH,
        )
        copy.start()
        return copy

    copies = []
    for k in range(1, CHUNKS):
        i, device = peer_a(k)
        copies.append(send(x_ref.at[i], first.at[k], s1.at[k], r1.at[k], device))
    total = x_ref[me_a]
    for k in range(1, CHUNKS):
        copies[k - 1].wait_recv()
        total = total + first[k]
    part[...] = total
    second[me_b] = total
    again = []
    for k in range(1, 8):
        j, device = peer_b(k)
        again.append(send(part, second.at[me_b], s2.at[k], r2.at[k], device))
    for copy in again:
        copy.wait_recv()
    total = second[0]
    for k in range(1, 8):
        total = total + second[k]
    res[me_a] = total
    last = []
    for k in range(1, CHUNKS):
        i, device = peer_a(k)
        last.append(send(res.at[me_a], res.at[me_a], s3.at[k], r3.at[k], device))
    for copy in last:
        copy.wait_recv()
    for i in range(8):
        gd_ref[MAIN * i : MAIN * (i + 1), :] = res[i, :MAIN, :C]
    whole = jnp.concatenate([res[8 + i, :MAIN, :] for i in range(8)], axis=0)
    gu_ref[...] = jnp.transpose(whole)[:C, :]
    low_ref[...] = jnp.concatenate([res[i, MAIN:, :] for i in range(7)], axis=1)
    for copy in copies + again + last:
        copy.wait_send()


def vmem(count):
    return [pl.BlockSpec(memory_space=pltpu.VMEM)] * count


def local(
    pixels,
    tissue,
    neighbours,
    upstream,
    stem_weight,
    stem_gain,
    dw_weight,
    norm_gain,
    up_weight,
    down_weight,
    layer_scale,
):
    tiles = lax.axis_size("tile")
    loss_factor = (tiles * lax.axis_size("slab") * SLOTS * SIDE * SIDE) ** (-0.5)
    cells, received = pl.pallas_call(
        functools.partial(stem_kernel, tiles),
        out_shape=(
            jax.ShapeDtypeStruct((SIDE, C, LANES), BF16),
            jax.ShapeDtypeStruct((2 * REACH + 2, RIM, C, LANES), BF16),
        ),
        in_specs=vmem(3),
        out_specs=tuple(vmem(2)),
        scratch_shapes=[
            pltpu.VMEM((2 * RIM, C, LANES), BF16),
            pltpu.SemaphoreType.DMA((2 * REACH + 2,)),
            pltpu.SemaphoreType.DMA((2 * REACH + 2,)),
        ],
        compiler_params=pltpu.CompilerParams(
            collective_id=0, has_side_effects=True, vmem_limit_bytes=48 * 1024 * 1024
        ),
        name="stem_exchange",
    )(pixels[0], stem_weight, stem_gain[None])

    taps = dw_weight.reshape(KS, KS, GROUPS, GROUP).transpose(2, 0, 1, 3)
    taps = jnp.pad(taps, ((0, 0), (0, 0), (0, TAPW // GROUP - KS), (0, 0))).reshape(GROUPS, BAND)
    tissue_t = tissue[0].reshape(LANES, SIDE).T.astype(F32).reshape(SIDE, 1, LANES)
    features, sums = pl.pallas_call(
        functools.partial(block_kernel, loss_factor),
        out_shape=(
            jax.ShapeDtypeStruct((LANES, SIDE * C), BF16),
            jax.ShapeDtypeStruct((CHUNKS, CHUNK_ROWS, 128), F32),
        ),
        in_specs=[pl.BlockSpec(memory_space=pltpu.SMEM)] + vmem(9),
        out_specs=tuple(vmem(2)),
        scratch_shapes=[
            pltpu.VMEM((KS, PADW, C, LANES), BF16),
            pltpu.VMEM((SIDE, C, LANES), BF16),
            pltpu.VMEM((2 * RIM, C, 2 * LANES), BF16),
            pltpu.VMEM((BLOCK, C, BLOCKS * LANES), F32),
            pltpu.VMEM((BLOCK, C, BLOCKS * LANES), BF16),
            pltpu.VMEM((SIDE, C, LANES), BF16),
            pltpu.VMEM((SIDE, C, LANES), BF16),
            pltpu.VMEM((HID, C), F32),
            pltpu.VMEM((HID, C), F32),
            pltpu.VMEM((C, LANES), F32),
            pltpu.VMEM((C, LANES), F32),
        ],
        compiler_params=pltpu.CompilerParams(vmem_limit_bytes=56 * 1024 * 1024),
        name="block",
    )(
        neighbours[0],
        cells,
        received,
        upstream.reshape(LANES, SIDE * C),
        tissue_t,
        taps,
        norm_gain[None],
        layer_scale[None],
        up_weight,
        down_weight,
    )

    dma = pltpu.SemaphoreType.DMA
    grad_down, grad_up, low = pl.pallas_call(
        reduce_kernel,
        out_shape=(
            jax.ShapeDtypeStruct((HID, C), F32),
            jax.ShapeDtypeStruct((C, HID), F32),
            jax.ShapeDtypeStruct((8, 7 * 128), F32),
        ),
        in_specs=vmem(1),
        out_specs=tuple(vmem(3)),
        scratch_shapes=[
            pltpu.VMEM((CHUNKS, CHUNK_ROWS, 128), F32),
            pltpu.VMEM((8, CHUNK_ROWS, 128), F32),
            pltpu.VMEM((CHUNK_ROWS, 128), F32),
            pltpu.VMEM((CHUNKS, CHUNK_ROWS, 128), F32),
            dma((CHUNKS,)),
            dma((CHUNKS,)),
            dma((8,)),
            dma((8,)),
            dma((CHUNKS,)),
            dma((CHUNKS,)),
        ],
        compiler_params=pltpu.CompilerParams(
            collective_id=1, has_side_effects=True, vmem_limit_bytes=48 * 1024 * 1024
        ),
        name="sum_gradients",
    )(sums)
    grad_dw = low[:GROUPS, : KS * KS * GROUP].reshape(GROUPS, KS * KS, GROUP).transpose(1, 0, 2)
    grad_dw = grad_dw.reshape(KS * KS, C)
    return (
        features.reshape(upstream.shape),
        grad_dw,
        low[GROUPS, :C],
        grad_up,
        grad_down,
        low[GROUPS + 1, :C],
    )


def solution(mesh):
    placed = (
        P("slab", "tile", None, None),
        P("slab", "tile", None),
        P("slab", "tile", None),
        P("slab", "tile", None, None),
        P(),
        P(),
        P(),
        P(),
        P(),
        P(),
        P(),
    )
    return jax.shard_map(
        local,
        mesh=mesh,
        in_specs=placed,
        out_specs=(P("slab", "tile", None, None), P(), P(), P(), P(), P()),
        check_vma=False,
    )
```

profile of v0, /device:TPU:1, one launch (start us, length us, event | category | flops | bytes accessed | tf_op | source)
XLA Modules:
  0.0 79.6 jit_solution(8310092382662386149)
XLA Ops:
  0.6 0.7 convert_element_type.11
  1.4 0.0 copy-start.6
  1.4 0.1 convert_element_type.12
  1.4 0.7 copy.21
  2.1 0.1 copy-done.6
  2.2 0.0 copy-start.7
  2.2 0.8 copy.23.down_ref
  3.0 0.0 copy-done.7
  3.0 0.1 reshape.36
  3.1 0.0 copy-start.3
  3.2 0.0 copy-start.4
  3.2 0.0 copy-start.5
  3.2 0.8 reshape.37.dw_ref
  4.0 0.2 copy-done.3
  4.1 0.0 copy-done.4
  4.1 0.0 copy-done.5
  4.1 20.0 %stem_exchange.1 = (bf16[32,96,128]{2,1,0:T(8,128)(2,1)S(1)}, bf16[12,3,96,128]{3,2,1,0:T(8,128)(2,1)S(1)}) custom-call(bf16[4,128,384]{2,1,0:T(8,128)(2,1)S(1)} %bitcast.18, bf16[48,96]{1,0:T(8,128)(2,1)S(1)} %copy-done.4, f32[1,96]{1,0:T(1,128)S(1)} %bitcast.20), custom_call_target="tpu_custom_call" | custom-call | tf_op jit(solution)/shard_map/stem_exchange/pallas_call | solution.py:480
  24.1 0.0 copy-start
  24.1 0.9 %copy-done = bf16[12,3,96,128]{3,2,1,0:T(8,128)(2,1)} copy-done((bf16[12,3,96,128]{3,2,1,0:T(8,128)(2,1)}, bf16[12,3,96,128]{3,2,1,0:T(8,128)(2,1)S(1)}, u32[]{:S(2)}) %copy-start) | copy-done | bytes 884760
  25.0 0.0 copy-start.1
  25.0 0.9 %copy-done.1 = bf16[32,96,128]{2,1,0:T(8,128)(2,1)} copy-done((bf16[32,96,128]{2,1,0:T(8,128)(2,1)}, bf16[32,96,128]{2,1,0:T(8,128)(2,1)S(1)}, u32[]{:S(2)}) %copy-start.1) | copy-done | bytes 786456
  26.0 21.9 %block.1 = (bf16[128,3072]{1,0:T(8,128)(2,1)}, f32[16,56,128]{2,1,0:T(8,128)}) custom-call(s32[4,8]{1,0:T(4,128)} %bitcast.26, bf16[32,96,128]{2,1,0:T(8,128)(2,1)} %copy-done.1, bf16[12,3,96,128]{3,2,1,0:T(8,128)(2,1)} %copy-done, bf16[128,3072]{1,0:T(8,128)(2,1)} %bitcast.22, f32[32,1,128]{2,1,0:T(1,128)} %bitcast.25, f32[6,1568]{1,0:T(8,128)} %reshape.37.dw_ref, ...), custom_call_target="tpu_custom_call" | custom-call | tf_op jit(solution)/shard_map/block/pallas_call | solution.py:502
  47.9 0.0 copy-start.2
  47.9 1.0 %copy-done.2 = f32[16,56,128]{2,1,0:T(8,128)S(1)} copy-done((f32[16,56,128]{2,1,0:T(8,128)S(1)}, f32[16,56,128]{2,1,0:T(8,128)}, u32[]{:S(2)}) %copy-start.2) | copy-done | bytes 458776
  48.9 27.8 %sum_gradients.1 = (f32[384,96]{1,0:T(8,128)S(1)}, f32[96,384]{1,0:T(8,128)S(1)}, f32[8,896]{1,0:T(8,128)S(1)}) custom-call(f32[16,56,128]{2,1,0:T(8,128)S(1)} %copy-done.2), custom_call_target="tpu_custom_call" | custom-call | tf_op jit(solution)/shard_map/sum_gradients/pallas_call | solution.py:539
  76.7 0.5 slice_bitcast_fusion
  77.2 0.8 copy.26
  78.0 0.1 reshape.39
  78.1 0.1 copy.24
  78.2 0.7 copy.25
  78.9 0.7 copy.29
  (2 shorter events, 0.1 us)
Async XLA Ops:
  1.4 0.9 %copy-start.6 = (bf16[384,96]{0,1:T(8,128)(2,1)S(1)}, bf16[384,96]{0,1:T(8,128)(2,1)}, u32[]{:S(2)}) copy-start(bf16[384,96]{0,1:T(8,128)(2,1)} %param.20) | copy-start | bytes 221188
  2.2 0.8 copy-start.7
  3.1 1.0 %copy-start.3 = (bf16[1,4,128,384]{3,2,1,0:T(8,128)(2,1)S(1)}, bf16[1,4,128,384]{3,2,1,0:T(8,128)(2,1)}, u32[]{:S(2)}) copy-start(bf16[1,4,128,384]{3,2,1,0:T(8,128)(2,1)} %param.11) | copy-start | bytes 1179652
  3.2 1.0 %copy-start.4 = (bf16[48,96]{1,0:T(8,128)(2,1)S(1)}, bf16[48,96]{1,0:T(8,128)(2,1)}, u32[]{:S(2)}) copy-start(bf16[48,96]{1,0:T(8,128)(2,1)} %w_ref.1) | copy-start | bytes 27652
  3.2 0.9 %copy-start.5 = (f32[96]{0:T(128)S(1)}, f32[96]{0:T(128)}, u32[]{:S(2)}) copy-start(f32[96]{0:T(128)} %param.16) | copy-start | bytes 1156
  24.1 0.9 %copy-start = (bf16[12,3,96,128]{3,2,1,0:T(8,128)(2,1)}, bf16[12,3,96,128]{3,2,1,0:T(8,128)(2,1)S(1)}, u32[]{:S(2)}) copy-start(bf16[12,3,96,128]{3,2,1,0:T(8,128)(2,1)S(1)} %get-tuple-element.14.recv_ref) | copy-start | bytes 2654212
  25.0 0.9 %copy-start.1 = (bf16[32,96,128]{2,1,0:T(8,128)(2,1)}, bf16[32,96,128]{2,1,0:T(8,128)(2,1)S(1)}, u32[]{:S(2)}) copy-start(bf16[32,96,128]{2,1,0:T(8,128)(2,1)S(1)} %get-tuple-element.13.ct_ref) | copy-start | bytes 2359300
  47.9 1.0 %copy-start.2 = (f32[16,56,128]{2,1,0:T(8,128)S(1)}, f32[16,56,128]{2,1,0:T(8,128)}, u32[]{:S(2)}) copy-start(f32[16,56,128]{2,1,0:T(8,128)} %get-tuple-element.16.x_ref) | copy-start | bytes 1376260
where the time goes:
time: 79.9 us; the launch traced here: 79.6 us
  Pallas kernels  69.6 us (87%)
  local copies, waits for them, and re-layouts  8.47 us (11%)
    pallas_call x1, Pallas kernels, local(): pl.pallas_call(reduce_kernel, out_shape=(jax.ShapeDtypeStruct((HID, C), F...  27.8 us
    pallas_call x1, Pallas kernels, local(): pl.pallas_call(functools.partial(block_kernel, loss_factor), out_shape=(j...  21.9 us
    pallas_call x1, Pallas kernels, local(): pl.pallas_call(functools.partial(stem_kernel, tiles), out_shape=(jax.Shap...  20 us
    unnamed x21, local copies, waits for them, and re-layouts  6.07 us

commit v1 on v0

v1 whole, which is shorter than its diff:
```python
import functools

import jax
import jax.numpy as jnp
from jax import lax
from jax.experimental import pallas as pl
from jax.experimental.pallas import tpu as pltpu
from jax.sharding import PartitionSpec as P

MESH = pl.DeviceIdType.MESH
C = 96
HID = 384
PATCH = 4
KS = 7
SIDE = 32
RIM = 3
REACH = 5
SLOTS = 4
LANES = SLOTS * SIDE
PADW = SIDE + 2 * RIM
GROUP = 16
GROUPS = C // GROUP
BLOCK = 8
BLOCKS = SIDE // BLOCK
TAPW = (BLOCK + RIM * 2) * GROUP
BAND = KS * TAPW
EPS = 1e-06
FILL_UNROLL = 32
STEP_UNROLL = 2
PLANE = 16
PIECE = HID // PLANE
PIECE_PAD = 32

BF16 = jnp.bfloat16
F32 = jnp.float32


def iota(shape, dim):
    return lax.broadcasted_iota(jnp.int32, shape, dim)


def onehot(mask):
    return jnp.where(mask, 1.0, 0.0).astype(BF16)


def mm(a, b):
    return lax.dot_general(a, b, (((1,), (0,)), ((), ())), preferred_element_type=F32)


def mm_nt(a, b):
    return lax.dot_general(a, b, (((1,), (1,)), ((), ())), preferred_element_type=F32)


def column(row, lanes):
    return jnp.transpose(jnp.broadcast_to(row, (lanes, row.shape[1])))


def gelu_parts(hidden):
    normal_cdf = 0.5 * (1.0 + lax.erf(hidden * 0.7071067811865476))
    density = jnp.exp(-0.5 * hidden * hidden) * 0.3989422804014327
    return (hidden * normal_cdf, normal_cdf + hidden * density)


def remote(source, target, send_sem, recv_sem, device):
    return pltpu.make_async_remote_copy(
        src_ref=source,
        dst_ref=target,
        send_sem=send_sem,
        recv_sem=recv_sem,
        device_id=device,
        device_id_type=MESH,
    )


def whole_kernel(
    tiles,
    loss_factor,
    nb_ref,
    pix_ref,
    stem_ref,
    stem_gain_ref,
    up_stream_ref,
    tissue_ref,
    dw_ref,
    gain_ref,
    up_ref,
    down_t_ref,
    scale_ref,
    feat_ref,
    out_dw_ref,
    out_gain_ref,
    out_up_ref,
    out_down_ref,
    out_scale_ref,
    ct_ref,
    strip_ref,
    recv_ref,
    pt_ref,
    ht_ref,
    side_ref,
    band_ref,
    mixed_ref,
    gm_ref,
    ut_ref,
    ft_ref,
    ts_ref,
    acc_ref,
    gg_ref,
    gs_ref,
    big_ref,
    core_in,
    rs_src,
    rs_in,
    y_buf,
    ag_buf,
    small_core,
    small_plane,
    small_y,
    send_sem,
    recv_sem,
    sum_send,
    sum_recv,
):
    me = lax.axis_index("tile")
    slab = lax.axis_index("slab")
    core = slab % 2
    y_hi = slab // 2
    me_plane = me % PLANE
    y_lo = me // PLANE
    me_y = y_lo + 2 * y_hi

    partner = {"tile": me, "slab": 2 * y_hi + (1 - core)}

    def plane_peer(k):
        i = lax.rem(me_plane + k, PLANE)
        return i, {"tile": y_lo * PLANE + i, "slab": slab}

    def y_peer(k):
        other_lo = lax.rem(y_lo + k % 2, 2)
        other_hi = lax.rem(y_hi + k // 2, 2)
        return {"tile": other_lo * PLANE + me_plane, "slab": 2 * other_hi + core}

    barrier = pltpu.get_barrier_semaphore()
    greeted = [
        {"tile": lax.rem(me + sign * d + tiles, tiles)} for d in range(1, REACH + 1) for sign in (-1, 1)
    ]
    greeted += [partner]
    greeted += [plane_peer(k)[1] for k in range(1, PLANE)]
    greeted += [y_peer(k) for k in range(1, 4)]
    for device in greeted:
        pl.semaphore_signal(barrier, inc=1, device_id=device, device_id_type=MESH)

    pix = pix_ref[...].reshape(SLOTS * SIDE * PATCH, SIDE * PATCH * 3)
    rows = SLOTS * SIDE * PATCH
    k_at, n_at = iota((rows, rows), 0), iota((rows, rows), 1)
    pick = onehot(k_at == PATCH * (n_at % LANES) + n_at // LANES)
    pix_t = mm(jnp.transpose(pix), pick).astype(BF16)

    q = PATCH * 3
    wt = jnp.transpose(stem_ref[...])
    k_at, n_at = iota((PATCH * q, PATCH * 4 * q), 0), iota((PATCH * q, PATCH * 4 * q), 1)
    spread_q = onehot((k_at // q == n_at // (4 * q)) & (k_at % q == n_at % q))
    wide = mm(wt, spread_q)
    wide = jnp.concatenate([wide] * 4, axis=0)
    r_at, n_at = iota(wide.shape, 0), iota(wide.shape, 1)
    block_w = jnp.where(r_at // C == (n_at % (4 * q)) // q, wide, 0.0).astype(BF16)

    stem_gain = column(stem_gain_ref[...], LANES)
    eight = SIDE // 4
    operand = jnp.concatenate(
        [
            jnp.concatenate(
                [pix_t[4 * q * g : 4 * q * (g + 1), LANES * pr : LANES * (pr + 1)] for pr in range(PATCH)],
                axis=0,
            )
            for g in range(eight)
        ],
        axis=1,
    )
    raw = mm(block_w, operand)
    for v in range(4):
        part = raw[C * v : C * (v + 1)]
        mean = jnp.sum(part, axis=0, keepdims=True) * (1.0 / C)
        part = part - mean
        inverse = lax.rsqrt(jnp.sum(part * part, axis=0, keepdims=True) * (1.0 / C) + EPS)
        part = part * inverse
        for g in range(eight):
            ct_ref[4 * g + v] = (part[:, LANES * g : LANES * (g + 1)] * stem_gain).astype(BF16)

    k_at, n_at = iota((LANES, 6 * LANES), 0), iota((LANES, 6 * LANES), 1)
    kind = n_at // LANES
    row_at = jnp.where(kind < RIM, kind, SIDE - 2 * RIM + kind)
    base = onehot((k_at // SIDE == n_at % SLOTS) & (k_at % SIDE == row_at))
    col_of = (n_at % LANES) // SLOTS
    packed = jnp.zeros((C, 6 * LANES), F32)
    for w in range(0, SIDE, 8):
        left = jnp.concatenate([ct_ref[w + i] for i in range(8)], axis=1)
        right = jnp.concatenate(
            [jnp.where(col_of == w + i, base, jnp.zeros_like(base)) for i in range(8)], axis=0
        )
        packed = packed + mm(left, right)
    for i in range(6):
        strip_ref[i] = packed[:, LANES * i : LANES * (i + 1)].astype(BF16)

    pl.semaphore_wait(barrier, len(greeted))
    strips_sent, sides_sent = [], []
    for d in range(1, REACH + 1):
        back = lax.rem(me - d + tiles, tiles)
        ahead = lax.rem(me + d, tiles)
        if d == 1:
            strips_sent.append((strip_ref.at[pl.ds(0, RIM)], 10, back))
            strips_sent.append((strip_ref.at[pl.ds(RIM, RIM)], 11, ahead))
        sides_sent.append((ct_ref.at[pl.ds(0, RIM)], d - 1, back))
        sides_sent.append((ct_ref.at[pl.ds(SIDE - RIM, RIM)], REACH + d - 1, ahead))

    def launch(copies):
        started = []
        for source, at, peer in copies:
            copy = remote(source, recv_ref.at[at], send_sem.at[at], recv_sem.at[at], {"tile": peer})
            copy.start()
            started.append(copy)
        return started

    strips_sent = launch(strips_sent)
    sides_sent = launch(sides_sent)

    tissue = tissue_ref[...].astype(F32)
    spread_rows = jnp.concatenate(
        [jnp.broadcast_to(tissue[t : t + 1], (SIDE, SIDE * SIDE)) for t in range(SLOTS)], axis=0
    )
    r_at, n_at = iota(spread_rows.shape, 0), iota(spread_rows.shape, 1)
    spread_rows = jnp.where(r_at % SIDE == n_at // SIDE, spread_rows, 0.0).astype(BF16)
    k_at, n_at = iota((SIDE, SIDE * SIDE), 0), iota((SIDE, SIDE * SIDE), 1)
    tissue_t = mm_nt(onehot(k_at == n_at % SIDE), spread_rows)
    for w in range(SIDE):
        ts_ref[w] = tissue_t[w : w + 1]

    for w in range(0, SIDE, 4):
        part = jnp.transpose(up_stream_ref[:, C * w : C * (w + 4)])
        for i in range(4):
            ut_ref[w + i] = part[C * i : C * (i + 1)]

    taps_t = jnp.transpose(dw_ref[...]).astype(BF16)
    k_at, n_at = iota((KS * KS, BAND), 0), iota((KS * KS, BAND), 1)
    col_at = (n_at % TAPW) // GROUP
    place = onehot((col_at < KS) & (k_at == KS * (n_at // TAPW) + col_at))
    taps = mm(taps_t, place)
    r_at, n_at = iota((GROUP, BAND), 0), iota((GROUP, BAND), 1)
    diagonal = r_at == n_at % GROUP
    for g in range(GROUPS):
        first = jnp.where(diagonal, taps[GROUP * g : GROUP * (g + 1)], 0.0).astype(BF16)
        band_ref[g, :GROUP, :] = first
        for w in range(1, BLOCK):
            band_ref[g, GROUP * w : GROUP * (w + 1), :] = pltpu.roll(first, GROUP * w, 1)

    lane = iota((1, LANES), 1)
    slot_of, row_of = lane // SIDE, lane % SIDE

    def per_tile(direction, rule):
        out = []
        for t in range(SLOTS):
            n = nb_ref[t, direction]
            out.append(jnp.where(n >= 0, rule(jnp.maximum(n, 0)), -1))
        return out

    def spread(values, shift):
        result = jnp.full((1, LANES), -1, jnp.int32)
        for t in range(SLOTS):
            result = jnp.where(slot_of == (t + shift) % SLOTS, values[t], result)
        return result

    def add_row(index, row):
        return jnp.where(index >= 0, index + row, -1)

    top = row_of >= SIDE - RIM
    bottom = row_of < RIM

    def own_rule(n):
        return jnp.where(n // SLOTS == me, (n % SLOTS) * SIDE, -1)

    def other_rule(n):
        return jnp.where(n // SLOTS == me, -1, n % SLOTS)

    own_above = spread(per_tile(0, own_rule), -1)
    own_below = spread(per_tile(1, own_rule), 1)
    own = add_row(jnp.where(top, own_above, jnp.where(bottom, own_below, -1)), row_of)
    select_own = onehot(iota((LANES, LANES), 0) == own)
    for w in range(0, SIDE, 8):
        near = mm(jnp.concatenate([ct_ref[w + i] for i in range(8)], axis=0), select_own).astype(BF16)
        for i in range(8):
            ht_ref[w + i] = near[C * i : C * (i + 1)]

    far_above = spread(per_tile(0, other_rule), -1)
    far_below = spread(per_tile(1, other_rule), 1)
    far = jnp.where(
        top,
        jnp.where(far_above >= 0, (row_of - (SIDE - RIM)) * SLOTS + far_above, -1),
        jnp.where(bottom & (far_below >= 0), (RIM + row_of) * SLOTS + far_below, -1),
    )
    k_at = iota((2 * RIM * LANES, LANES), 0)
    far_base = onehot((k_at // LANES) * SLOTS + k_at % SLOTS == far)
    col_of = (k_at % LANES) // SLOTS

    up_w = up_ref[...]
    down_t = down_t_ref[...]
    up_t = jnp.transpose(up_w)
    down_w = jnp.transpose(down_t)
    gain = column(gain_ref[...], LANES)
    scale = column(scale_ref[...], LANES)
    gain = jnp.concatenate([gain] * 4, axis=1)
    scale = jnp.concatenate([scale] * 4, axis=1)
    acc_ref[...] = jnp.zeros_like(acc_ref)
    gg_ref[...] = jnp.zeros_like(gg_ref)
    gs_ref[...] = jnp.zeros_like(gs_ref)

    for copy in strips_sent:
        copy.wait()
    strips = jnp.concatenate(
        [recv_ref[11, i] for i in range(RIM)] + [recv_ref[10, i] for i in range(RIM)], axis=1
    )
    for w in range(0, SIDE, 4):
        select_far = jnp.concatenate(
            [jnp.where(col_of == w + i, far_base, jnp.zeros_like(far_base)) for i in range(4)], axis=1
        )
        got = mm(strips, select_far).astype(BF16)
        for i in range(4):
            ht_ref[w + i] = ht_ref[w + i] + got[:, LANES * i : LANES * (i + 1)]

    def fill(at, centre, halo):
        for a in range(KS):
            s = a - RIM
            if s > 0:
                value = pltpu.roll(jnp.where(row_of < s, halo, centre), LANES - s, 1)
            elif s < 0:
                value = pltpu.roll(jnp.where(row_of >= SIDE + s, halo, centre), -s, 1)
            else:
                value = centre
            pt_ref[a, at] = value

    def fill_step(w, carry):
        fill(RIM + w, ct_ref[w], ht_ref[w])
        return carry

    lax.fori_loop(0, SIDE, fill_step, 0, unroll=FILL_UNROLL)

    def window(g, blocks):
        return jnp.concatenate(
            [
                jnp.concatenate(
                    [
                        pt_ref[a, BLOCK * j : BLOCK * j + TAPW // GROUP, GROUP * g : GROUP * (g + 1)].reshape(
                            TAPW, LANES
                        )
                        for a in range(KS)
                    ],
                    axis=0,
                )
                for j in blocks
            ],
            axis=1,
        )

    def fold(values):
        total = values[:, :LANES]
        for j in range(1, values.shape[1] // LANES):
            total = total + values[:, LANES * j : LANES * (j + 1)]
        return total

    def work(blocks):
        for g in range(GROUPS):
            out = mm(band_ref[g], window(g, blocks))
            for w in range(BLOCK):
                mixed_ref[w, GROUP * g : GROUP * (g + 1), :] = out[GROUP * w : GROUP * (w + 1)]

        def step(i, carry):
            columns = [(2 * i + v, j) for v in range(2) for j in blocks]

            def gather(ref):
                return jnp.concatenate([ref[BLOCK * j + w] for w, j in columns], axis=1)

            mixed = jnp.concatenate([mixed_ref[2 * i], mixed_ref[2 * i + 1]], axis=1)
            mean = jnp.sum(mixed, axis=0, keepdims=True) * (1.0 / C)
            centered = mixed - mean
            inverse = lax.rsqrt(jnp.sum(centered * centered, axis=0, keepdims=True) * (1.0 / C) + EPS)
            normed = centered * inverse
            lowered = (normed * gain).astype(BF16)
            hidden = mm(up_t, lowered)
            active, steepness = gelu_parts(hidden)
            active = active.astype(BF16)
            branch = mm(down_t, active)
            tissue = gather(ts_ref)
            summed = gather(ct_ref).astype(F32) + scale * branch
            features = (summed * tissue).astype(BF16)
            grad_out = gather(ut_ref).astype(F32) * (tissue * loss_factor)
            gs_ref[...] += fold(grad_out * branch)
            grad_branch = (grad_out * scale).astype(BF16)
            acc_ref[0] += mm_nt(active, grad_branch)
            grad_active = mm(down_w, grad_branch)
            grad_hidden = (grad_active * steepness).astype(BF16)
            acc_ref[1] += mm_nt(grad_hidden, lowered)
            grad_lowered = mm(up_w, grad_hidden)
            gg_ref[...] += fold(grad_lowered * normed)
            scaled = grad_lowered * gain
            mean_one = jnp.sum(scaled, axis=0, keepdims=True) * (1.0 / C)
            mean_two = jnp.sum(scaled * normed, axis=0, keepdims=True) * (1.0 / C)
            grad_mixed = (inverse * (scaled - mean_one - normed * mean_two)).astype(BF16)
            for at, (w, j) in enumerate(columns):
                lanes = slice(LANES * at, LANES * (at + 1))
                gm_ref[w, :, LANES * j : LANES * (j + 1)] = grad_mixed[:, lanes]
                ft_ref[BLOCK * j + w] = features[:, lanes]
            return carry

        lax.fori_loop(0, BLOCK // 2, step, 0, unroll=STEP_UNROLL)

    work((1, 2))

    for copy in sides_sent:
        copy.wait()
    for east in (0, 1):
        def rule(n, east=east):
            away = n // SLOTS - me
            away = away if east else -away
            return away * LANES + (n % SLOTS) * SIDE

        straight = spread(per_tile(2 + east, rule), 0)
        above = spread(per_tile(4 + east, rule), -1)
        below = spread(per_tile(6 + east, rule), 1)
        halo = jnp.where(top, above, jnp.where(bottom, below, -1))
        index = jnp.concatenate([add_row(straight, row_of), add_row(halo, row_of)], axis=1)
        select = onehot(iota(((REACH + 1) * LANES, 2 * LANES), 0) == index)
        first = 0 if east else SIDE - RIM
        base = 0 if east else REACH
        source = jnp.concatenate(
            [
                jnp.concatenate(
                    [ct_ref[first + i]] + [recv_ref[base + d, i] for d in range(REACH)], axis=1
                )
                for i in range(RIM)
            ],
            axis=0,
        )
        sides = mm(source, select).astype(BF16)
        for i in range(RIM):
            side_ref[east * RIM + i] = sides[C * i : C * (i + 1)]

    for i in range(RIM):
        for east in (0, 1):
            both = side_ref[east * RIM + i]
            fill(east * (RIM + SIDE) + i, both[:, :LANES], both[:, LANES:])

    work((0, 3))

    def pieces(values):
        filled = jnp.concatenate([values, jnp.zeros((HID, 128 - C), F32)], axis=1)
        out = []
        for i in range(PLANE):
            piece = filled[PIECE * i : PIECE * (i + 1)]
            out.append(jnp.concatenate([piece, jnp.zeros((PIECE_PAD - PIECE, 128), F32)], axis=0))
        return out

    for half in range(2):
        for i, piece in enumerate(pieces(acc_ref[half])):
            big_ref[half, i] = piece.astype(BF16)
    to_core = remote(big_ref.at[1 - core], core_in, sum_send.at[0], sum_recv.at[0], partner)
    to_core.start()

    def gradient(g):
        left = jnp.concatenate([gm_ref[w, GROUP * g : GROUP * (g + 1), :] for w in range(BLOCK)], axis=0)
        full = mm_nt(left, window(g, range(BLOCKS)))
        total = None
        for w in range(BLOCK):
            part = jnp.where(diagonal, full[GROUP * w : GROUP * (w + 1)], 0.0)
            if w:
                part = pltpu.roll(part, BAND - GROUP * w, 1)
            total = part if total is None else total + part
        return total

    totals = [gradient(g) for g in range(GROUPS // 2)]

    to_core.wait()
    for i in range(PLANE):
        rs_src[i] = (big_ref[core, i].astype(F32) + core_in[i].astype(F32)).astype(BF16)

    def scatter(target, source, at):
        for k in range(1, PLANE):
            i, device = plane_peer(k)
            remote(source(i), target(k), sum_send.at[at], sum_recv.at[at], device).start()

    def settle(ref, count, at):
        block = ref.at[pl.ds(0, count)]
        copy = remote(block, block, sum_send.at[at], sum_recv.at[at], partner)
        copy.wait()

    scatter(lambda k: rs_in.at[k], lambda i: rs_src.at[i], 1)

    totals += [gradient(g) for g in range(GROUPS // 2, GROUPS)]
    totals = jnp.concatenate(totals, axis=0).astype(BF16)
    k_at, n_at = iota((BAND, LANES), 0), iota((BAND, LANES), 1)
    col_at = (k_at % TAPW) // GROUP
    place = onehot((col_at < KS) & (n_at == KS * (k_at // TAPW) + col_at))
    small = mm(totals, place)
    n_at = iota((C, LANES), 1)
    small = jnp.where(n_at == KS * KS, jnp.sum(gg_ref[...], axis=1, keepdims=True), small)
    small = jnp.where(n_at == KS * KS + 1, jnp.sum(gs_ref[...], axis=1, keepdims=True), small)
    small = jnp.concatenate([small[: C // 2, :64], small[C // 2 :, :64]], axis=1).astype(BF16)
    small_core[core] = small
    small_to_core = remote(
        small_core.at[core], small_core.at[core], sum_send.at[2], sum_recv.at[2], partner
    )
    small_to_core.start()
    small_to_core.wait()
    small = (small_core[0].astype(F32) + small_core[1].astype(F32)).astype(BF16)
    small_plane[me_plane] = small
    scatter(lambda k: small_plane.at[me_plane], lambda i: small_plane.at[me_plane], 3)

    settle(rs_in, PLANE - 1, 1)
    total = rs_src[me_plane].astype(F32)
    for k in range(1, PLANE):
        total = total + rs_in[k].astype(F32)
    y_buf[me_y] = total.astype(BF16)
    for k in range(1, 4):
        remote(y_buf.at[me_y], y_buf.at[me_y], sum_send.at[4], sum_recv.at[4], y_peer(k)).start()

    settle(small_plane, PLANE - 1, 3)
    total = small_plane[0].astype(F32)
    for k in range(1, PLANE):
        total = total + small_plane[k].astype(F32)
    small_y[me_y] = total.astype(BF16)
    for k in range(1, 4):
        remote(small_y.at[me_y], small_y.at[me_y], sum_send.at[5], sum_recv.at[5], y_peer(k)).start()

    settle(y_buf, 3, 4)
    total = y_buf[0].astype(F32)
    for k in range(1, 4):
        total = total + y_buf[k].astype(F32)
    ag_buf[core, me_plane] = total.astype(BF16)
    scatter(lambda k: ag_buf.at[core, me_plane], lambda i: ag_buf.at[core, me_plane], 6)

    for w in range(0, SIDE, 4):
        part = jnp.concatenate([ft_ref[w + i] for i in range(4)], axis=0)
        feat_ref[:, C * w : C * (w + 4)] = jnp.transpose(part)

    settle(small_y, 3, 5)
    total = small_y[0].astype(F32)
    for k in range(1, 4):
        total = total + small_y[k].astype(F32)
    total = jnp.concatenate([total[:, :64], total[:, 64:]], axis=0)
    total = jnp.transpose(jnp.concatenate([total, jnp.zeros((C, 64), F32)], axis=1))
    out_dw_ref[...] = total[: KS * KS]
    out_gain_ref[...] = total[KS * KS : KS * KS + 1]
    out_scale_ref[...] = total[KS * KS + 1 : KS * KS + 2]

    settle(ag_buf.at[core], PLANE - 1, 6)
    last = remote(ag_buf.at[core], ag_buf.at[core], sum_send.at[7], sum_recv.at[7], partner)
    last.start()
    last.wait()
    for half, ref in ((0, out_down_ref), (1, out_up_ref)):
        joined = jnp.concatenate([ag_buf[half, i].astype(F32)[:PIECE] for i in range(PLANE)], axis=0)
        ref[...] = jnp.transpose(joined)[:C]


def vmem(count):
    return [pl.BlockSpec(memory_space=pltpu.VMEM)] * count


def local(
    pixels,
    tissue,
    neighbours,
    upstream,
    stem_weight,
    stem_gain,
    dw_weight,
    norm_gain,
    up_weight,
    down_weight,
    layer_scale,
):
    tiles = lax.axis_size("tile")
    loss_factor = (tiles * lax.axis_size("slab") * SLOTS * SIDE * SIDE) ** (-0.5)
    dma = pltpu.SemaphoreType.DMA
    features, grad_dw, grad_gain, grad_up, grad_down_t, grad_scale = pl.pallas_call(
        functools.partial(whole_kernel, tiles, loss_factor),
        out_shape=(
            jax.ShapeDtypeStruct((LANES, SIDE * C), BF16),
            jax.ShapeDtypeStruct((KS * KS, C), F32),
            jax.ShapeDtypeStruct((1, C), F32),
            jax.ShapeDtypeStruct((C, HID), F32),
            jax.ShapeDtypeStruct((C, HID), F32),
            jax.ShapeDtypeStruct((1, C), F32),
        ),
        in_specs=[pl.BlockSpec(memory_space=pltpu.SMEM)] + vmem(10),
        out_specs=tuple(vmem(6)),
        scratch_shapes=[
            pltpu.VMEM((SIDE, C, LANES), BF16),
            pltpu.VMEM((2 * RIM, C, LANES), BF16),
            pltpu.VMEM((2 * REACH + 2, RIM, C, LANES), BF16),
            pltpu.VMEM((KS, PADW, C, LANES), BF16),
            pltpu.VMEM((SIDE, C, LANES), BF16),
            pltpu.VMEM((2 * RIM, C, 2 * LANES), BF16),
            pltpu.VMEM((GROUPS, BLOCK * GROUP, BAND), BF16),
            pltpu.VMEM((BLOCK, C, 2 * LANES), F32),
            pltpu.VMEM((BLOCK, C, BLOCKS * LANES), BF16),
            pltpu.VMEM((SIDE, C, LANES), BF16),
            pltpu.VMEM((SIDE, C, LANES), BF16),
            pltpu.VMEM((SIDE, 1, LANES), F32),
            pltpu.VMEM((2, HID, C), F32),
            pltpu.VMEM((C, LANES), F32),
            pltpu.VMEM((C, LANES), F32),
            pltpu.VMEM((2, PLANE, PIECE_PAD, 128), BF16),
            pltpu.VMEM((PLANE, PIECE_PAD, 128), BF16),
            pltpu.VMEM((PLANE, PIECE_PAD, 128), BF16),
            pltpu.VMEM((PLANE, PIECE_PAD, 128), BF16),
            pltpu.VMEM((4, PIECE_PAD, 128), BF16),
            pltpu.VMEM((2, PLANE, PIECE_PAD, 128), BF16),
            pltpu.VMEM((2, C // 2, 128), BF16),
            pltpu.VMEM((PLANE, C // 2, 128), BF16),
            pltpu.VMEM((4, C // 2, 128), BF16),
            dma((2 * REACH + 2,)),
            dma((2 * REACH + 2,)),
            dma((8,)),
            dma((8,)),
        ],
        compiler_params=pltpu.CompilerParams(
            collective_id=0, has_side_effects=True, vmem_limit_bytes=56 * 1024 * 1024
        ),
        name="whole",
    )(
        neighbours[0],
        pixels[0],
        stem_weight,
        stem_gain[None],
        upstream.reshape(LANES, SIDE * C),
        tissue[0],
        dw_weight,
        norm_gain[None],
        up_weight,
        down_weight.T,
        layer_scale[None],
    )
    return (
        features.reshape(upstream.shape),
        grad_dw,
        grad_gain[0],
        grad_up,
        grad_down_t.T,
        grad_scale[0],
    )


def solution(mesh):
    placed = (
        P("slab", "tile", None, None),
        P("slab", "tile", None),
        P("slab", "tile", None),
        P("slab", "tile", None, None),
        P(),
        P(),
        P(),
        P(),
        P(),
        P(),
        P(),
    )
    return jax.shard_map(
        local,
        mesh=mesh,
        in_specs=placed,
        out_specs=(P("slab", "tile", None, None), P(), P(), P(), P(), P()),
        check_vma=False,
    )
```

time: 79.9 us -> 53.1 us (0.66)
  Pallas kernels: 69.6 us -> 46.8 us
  local copies, waits for them, and re-layouts: 8.47 us -> 5.39 us
    pallas_call x3 -> x1, Pallas kernels: 69.6 us -> 46.8 us  [local(): pl.pallas_call(functools.partial(whole_kernel, tiles, loss_factor), out_s...]
    reshape x3 -> x0, local copies, waits for them, and re-layouts: 0.98 us -> none  [the longest x1 0.78 us: local(): jnp.pad(taps, ((0, 0), (0, 0), (0, TAPW // GROUP - KS), (0, 0)))]
    unnamed x21 -> x16, local copies, waits for them, and re-layouts: 6.07 us -> 5.39 us
where the time goes in v1:
time: 53.1 us; the launch traced here: 52.9 us
  Pallas kernels  46.8 us (88%)
  local copies, waits for them, and re-layouts  5.39 us (10%)
  between operations  0.67 us (1%)
    pallas_call x1, Pallas kernels, local(): pl.pallas_call(functools.partial(whole_kernel, tiles, loss_factor), out_s...  46.8 us
    unnamed x16, local copies, waits for them, and re-layouts  5.39 us

profile of v1, /device:TPU:1, one launch (start us, length us, event | category | flops | bytes accessed | tf_op | source)
XLA Modules:
  0.0 52.9 jit_solution(16613344159997677775)
XLA Ops:
  0.6 46.8 %whole.1 = (bf16[128,3072]{1,0:T(8,128)(2,1)}, f32[49,96]{1,0:T(8,128)}, f32[1,96]{1,0:T(1,128)}, f32[96,384]{1,0:T(8,128)}, f32[96,384]{1,0:T(8,128)}, /*index=5*/f32[1,96]{1,0:T(1,128)}) custom-call(s32[4,8]{1,0:T(4,128)} %bitcast.18, bf16[4,128,384]{2,1,0:T(8,128)(2,1)} %bitcast.14, bf16[48,96]{1,0:T(8,128)(2,1)} %stem_ref.1, f32[1,96]{1,0:T(1,128)} %bitcast.19, ...), custom_call_target="tpu_custom_call" | custom-call | tf_op jit(solution)/shard_map/whole/pallas_call | solution.py:582
  47.4 0.0 copy-start.2
  47.5 0.0 copy-start.1
  47.5 2.1 %copy.23 = bf16[1,4,32,3072]{3,2,1,0:T(8,128)(2,1)} copy(bf16[1,4,32,3072]{3,2,1,0:T(8,128)(2,1)} %bitcast.13) | data formatting | bytes 1572864
  49.6 0.0 copy-done.2
  49.6 0.0 copy-start.4
  49.6 0.6 %copy.24 = f32[49,96]{1,0:T(8,128)} copy(f32[49,96]{1,0:T(8,128)S(1)} %copy-done.2) | data formatting | bytes 37632
  50.2 0.0 copy-done.4
  50.2 0.5 copy.25
  50.7 0.0 copy-done.1
  50.7 0.0 copy-start
  50.7 0.7 %copy.26 = f32[96,384]{1,0:T(8,128)} copy(f32[96,384]{1,0:T(8,128)S(1)} %copy-done.1) | data formatting | bytes 294912
  51.4 0.3 copy-done
  51.7 0.0 copy-start.3
  51.7 0.7 %copy.27 = f32[384,96]{0,1:T(8,128)} copy(f32[384,96]{0,1:T(8,128)S(1)} %bitcast.15) | data formatting | bytes 294912
  52.3 0.0 copy-done.3
  52.4 0.5 copy.28
Async XLA Ops:
  47.4 2.1 %copy-start.2 = (f32[49,96]{1,0:T(8,128)S(1)}, f32[49,96]{1,0:T(8,128)}, u32[]{:S(2)}) copy-start(f32[49,96]{1,0:T(8,128)} %get-tuple-element.25) | copy-start | bytes 56452
  47.5 3.3 %copy-start.1 = (f32[96,384]{1,0:T(8,128)S(1)}, f32[96,384]{1,0:T(8,128)}, u32[]{:S(2)}) copy-start(f32[96,384]{1,0:T(8,128)} %get-tuple-element.27) | copy-start | bytes 442372
  49.6 0.6 %copy-start.4 = (f32[1,96]{1,0:T(1,128)S(1)}, f32[1,96]{1,0:T(1,128)}, u32[]{:S(2)}) copy-start(f32[1,96]{1,0:T(1,128)} %get-tuple-element.14) | copy-start | bytes 1156
  50.7 1.0 %copy-start = (f32[96,384]{1,0:T(8,128)S(1)}, f32[96,384]{1,0:T(8,128)}, u32[]{:S(2)}) copy-start(f32[96,384]{1,0:T(8,128)} %get-tuple-element.16) | copy-start | bytes 442372
  51.7 0.7 %copy-start.3 = (f32[1,96]{1,0:T(1,128)S(1)}, f32[1,96]{1,0:T(1,128)}, u32[]{:S(2)}) copy-start(f32[1,96]{1,0:T(1,128)} %get-tuple-element.17) | copy-start | bytes 1156

commit v2 on v1

--- a/solution.py
+++ b/solution.py
@@ -25,8 +25,8 @@
 TAPW = (BLOCK + RIM * 2) * GROUP
 BAND = KS * TAPW
 EPS = 1e-06
+VMEM_BYTES = 56 * 1024 * 1024
 FILL_UNROLL = 32
-STEP_UNROLL = 2
 PLANE = 16
 PIECE = HID // PLANE
 PIECE_PAD = 32
@@ -76,51 +76,57 @@
     tiles,
     loss_factor,
     nb_ref,
-    pix_ref,
-    stem_ref,
-    stem_gain_ref,
-    up_stream_ref,
-    tissue_ref,
-    dw_ref,
-    gain_ref,
-    up_ref,
-    down_t_ref,
-    scale_ref,
-    feat_ref,
-    out_dw_ref,
-    out_gain_ref,
-    out_up_ref,
-    out_down_ref,
-    out_scale_ref,
-    ct_ref,
-    strip_ref,
-    recv_ref,
-    pt_ref,
-    ht_ref,
-    side_ref,
-    band_ref,
-    mixed_ref,
-    gm_ref,
-    ut_ref,
-    ft_ref,
-    ts_ref,
-    acc_ref,
-    gg_ref,
-    gs_ref,
-    big_ref,
-    core_in,
-    rs_src,
-    rs_in,
-    y_buf,
-    ag_buf,
-    small_core,
-    small_plane,
-    small_y,
-    send_sem,
-    recv_sem,
-    sum_send,
-    sum_recv,
+    *refs,
 ):
+    inputs, refs = refs[:10], refs[10:]
+    (feat_ref, ag_out, small_out), refs = refs[:3], refs[3:]
+    held, refs = refs[:10], refs[10:]
+    (
+        pix_ref,
+        stem_ref,
+        stem_gain_ref,
+        up_vmem,
+        tissue_ref,
+        dw_ref,
+        gain_ref,
+        up_ref,
+        down_t_ref,
+        scale_ref,
+    ) = held
+    (
+        feat_vmem,
+        ag_buf,
+        small_ref,
+        ct_ref,
+        strip_ref,
+        strip_in,
+        recv_ref,
+        pt_ref,
+        ht_ref,
+        side_ref,
+        band_ref,
+        mixed_ref,
+        gm_ref,
+        ut_ref,
+        ft_ref,
+        ts_ref,
+        acc_ref,
+        gg_ref,
+        gs_ref,
+        big_ref,
+        core_in,
+        rs_src,
+        rs_in,
+        y_buf,
+        small_core,
+        small_plane,
+        small_y,
+        send_sem,
+        recv_sem,
+        sum_send,
+        sum_recv,
+        local_sem,
+    ) = refs
     me = lax.axis_index("tile")
     slab = lax.axis_index("slab")
     core = slab % 2
@@ -129,6 +135,12 @@
     y_lo = me // PLANE
     me_y = y_lo + 2 * y_hi
 
+    fetches = [
+        pltpu.make_async_copy(there, here, local_sem.at[i])
+        for i, (there, here) in enumerate(zip(inputs, held))
+    ]
+    for copy in fetches:
+        copy.start()
     partner = {"tile": me, "slab": 2 * y_hi + (1 - core)}
 
     def plane_peer(k):
@@ -150,6 +162,8 @@
     for device in greeted:
         pl.semaphore_signal(barrier, inc=1, device_id=device, device_id_type=MESH)
 
+    for copy in fetches[:3]:
+        copy.wait()
     pix = pix_ref[...].reshape(SLOTS * SIDE * PATCH, SIDE * PATCH * 3)
     rows = SLOTS * SIDE * PATCH
     k_at, n_at = iota((rows, rows), 0), iota((rows, rows), 1)
@@ -187,19 +201,29 @@
         for g in range(eight):
             ct_ref[4 * g + v] = (part[:, LANES * g : LANES * (g + 1)] * stem_gain).astype(BF16)
 
-    k_at, n_at = iota((LANES, 6 * LANES), 0), iota((LANES, 6 * LANES), 1)
-    kind = n_at // LANES
-    row_at = jnp.where(kind < RIM, kind, SIDE - 2 * RIM + kind)
-    base = onehot((k_at // SIDE == n_at % SLOTS) & (k_at % SIDE == row_at))
-    col_of = (n_at % LANES) // SLOTS
-    packed = jnp.zeros((C, 6 * LANES), F32)
+    tiles_here = 0
+    for t in range(SLOTS):
+        any_side = nb_ref[t, 0]
+        for direction in range(1, 8):
+            any_side = jnp.maximum(any_side, nb_ref[t, direction])
+        tiles_here = tiles_here + jnp.where(any_side >= 0, 1, 0)
+    k_at, n_at = iota((LANES, 2 * LANES), 0), iota((LANES, 2 * LANES), 1)
+    lower = n_at >= LANES
+    kind = (n_at % LANES) // SIDE
+    base = onehot(
+        (kind < RIM)
+        & (k_at // SIDE == jnp.where(lower, tiles_here - 1, 0))
+        & (k_at % SIDE == jnp.where(lower, SIDE - RIM + kind, kind))
+    )
+    col_of = n_at % SIDE
+    packed = jnp.zeros((C, 2 * LANES), F32)
     for w in range(0, SIDE, 8):
         left = jnp.concatenate([ct_ref[w + i] for i in range(8)], axis=1)
         right = jnp.concatenate(
             [jnp.where(col_of == w + i, base, jnp.zeros_like(base)) for i in range(8)], axis=0
         )
         packed = packed + mm(left, right)
-    for i in range(6):
+    for i in range(2):
         strip_ref[i] = packed[:, LANES * i : LANES * (i + 1)].astype(BF16)
 
     pl.semaphore_wait(barrier, len(greeted))
@@ -208,15 +232,16 @@
         back = lax.rem(me - d + tiles, tiles)
         ahead = lax.rem(me + d, tiles)
         if d == 1:
-            strips_sent.append((strip_ref.at[pl.ds(0, RIM)], 10, back))
-            strips_sent.append((strip_ref.at[pl.ds(RIM, RIM)], 11, ahead))
-        sides_sent.append((ct_ref.at[pl.ds(0, RIM)], d - 1, back))
-        sides_sent.append((ct_ref.at[pl.ds(SIDE - RIM, RIM)], REACH + d - 1, ahead))
+            strips_sent.append((strip_ref.at[0], strip_in.at[0], 10, back))
+            strips_sent.append((strip_ref.at[1], strip_in.at[1], 11, ahead))
+        sides_sent.append((ct_ref.at[pl.ds(0, RIM)], recv_ref.at[d - 1], d - 1, back))
+        at = REACH + d - 1
+        sides_sent.append((ct_ref.at[pl.ds(SIDE - RIM, RIM)], recv_ref.at[at], at, ahead))
 
     def launch(copies):
         started = []
-        for source, at, peer in copies:
-            copy = remote(source, recv_ref.at[at], send_sem.at[at], recv_sem.at[at], {"tile": peer})
+        for source, target, at, peer in copies:
+            copy = remote(source, target, send_sem.at[at], recv_sem.at[at], {"tile": peer})
             copy.start()
             started.append(copy)
         return started
@@ -224,6 +249,8 @@
     strips_sent = launch(strips_sent)
     sides_sent = launch(sides_sent)
 
+    for copy in fetches[3:]:
+        copy.wait()
     tissue = tissue_ref[...].astype(F32)
     spread_rows = jnp.concatenate(
         [jnp.broadcast_to(tissue[t : t + 1], (SIDE, SIDE * SIDE)) for t in range(SLOTS)], axis=0
@@ -236,7 +263,7 @@
         ts_ref[w] = tissue_t[w : w + 1]
 
     for w in range(0, SIDE, 4):
-        part = jnp.transpose(up_stream_ref[:, C * w : C * (w + 4)])
+        part = jnp.transpose(up_vmem[:, C * w : C * (w + 4)])
         for i in range(4):
             ut_ref[w + i] = part[C * i : C * (i + 1)]
 
@@ -279,7 +306,7 @@
         return jnp.where(n // SLOTS == me, (n % SLOTS) * SIDE, -1)
 
     def other_rule(n):
-        return jnp.where(n // SLOTS == me, -1, n % SLOTS)
+        return jnp.where(n // SLOTS == me, -1, 1)
 
     own_above = spread(per_tile(0, own_rule), -1)
     own_below = spread(per_tile(1, own_rule), 1)
@@ -293,13 +320,13 @@
     far_above = spread(per_tile(0, other_rule), -1)
     far_below = spread(per_tile(1, other_rule), 1)
     far = jnp.where(
-        top,
-        jnp.where(far_above >= 0, (row_of - (SIDE - RIM)) * SLOTS + far_above, -1),
-        jnp.where(bottom & (far_below >= 0), (RIM + row_of) * SLOTS + far_below, -1),
-    )
-    k_at = iota((2 * RIM * LANES, LANES), 0)
-    far_base = onehot((k_at // LANES) * SLOTS + k_at % SLOTS == far)
-    col_of = (k_at % LANES) // SLOTS
+        top & (far_above >= 0),
+        row_of - (SIDE - RIM),
+        jnp.where(bottom & (far_below >= 0), SLOTS + row_of, -1),
+    )
+    k_at = iota((2 * LANES, LANES), 0)
+    far_base = onehot(k_at // SIDE == far)
+    col_of = k_at % SIDE
 
     up_w = up_ref[...]
     down_t = down_t_ref[...]
@@ -315,9 +342,7 @@
 
     for copy in strips_sent:
         copy.wait()
-    strips = jnp.concatenate(
-        [recv_ref[11, i] for i in range(RIM)] + [recv_ref[10, i] for i in range(RIM)], axis=1
-    )
+    strips = jnp.concatenate([strip_in[1], strip_in[0]], axis=1)
     for w in range(0, SIDE, 4):
         select_far = jnp.concatenate(
             [jnp.where(col_of == w + i, far_base, jnp.zeros_like(far_base)) for i in range(4)], axis=1
@@ -366,18 +391,23 @@
             total = total + values[:, LANES * j : LANES * (j + 1)]
         return total
 
-    def work(blocks):
+    def work(blocks, defer):
         for g in range(GROUPS):
             out = mm(band_ref[g], window(g, blocks))
             for w in range(BLOCK):
                 mixed_ref[w, GROUP * g : GROUP * (g + 1), :] = out[GROUP * w : GROUP * (w + 1)]
 
-        def step(i, carry):
-            columns = [(2 * i + v, j) for v in range(2) for j in blocks]
-
-            def gather(ref):
-                return jnp.concatenate([ref[BLOCK * j + w] for w, j in columns], axis=1)
-
+        def pair_of(i):
+            return [(2 * i + v, j) for v in range(2) for j in blocks]
+
+        def gather(ref, i):
+            return jnp.concatenate([ref[BLOCK * j + w] for w, j in pair_of(i)], axis=1)
+
+        def front(i):
+            tissue = gather(ts_ref, i)
+            grad_out = gather(ut_ref, i).astype(F32) * (tissue * loss_factor)
+            grad_branch = (grad_out * scale).astype(BF16)
+            grad_active = mm(down_w, grad_branch)
             mixed = jnp.concatenate([mixed_ref[2 * i], mixed_ref[2 * i + 1]], axis=1)
             mean = jnp.sum(mixed, axis=0, keepdims=True) * (1.0 / C)
             centered = mixed - mean
@@ -385,34 +415,55 @@
             normed = centered * inverse
             lowered = (normed * gain).astype(BF16)
             hidden = mm(up_t, lowered)
+            return tissue, grad_out, grad_branch, grad_active, normed, inverse, lowered, hidden
+
+        def middle(state):
+            grad_active, hidden = state[3], state[7]
             active, steepness = gelu_parts(hidden)
-            active = active.astype(BF16)
+            return active.astype(BF16), (grad_active * steepness).astype(BF16)
+
+        def large(state, pair):
+            active, grad_hidden = pair
+            acc_ref[0] += mm_nt(active, state[2])
+            acc_ref[1] += mm_nt(grad_hidden, state[6])
+
+        def back(i, state, pair):
+            tissue, grad_out, _, _, normed, inverse, _, _ = state
+            active, grad_hidden = pair
+            grad_lowered = mm(up_w, grad_hidden)
             branch = mm(down_t, active)
-            tissue = gather(ts_ref)
-            summed = gather(ct_ref).astype(F32) + scale * branch
+            summed = gather(ct_ref, i).astype(F32) + scale * branch
             features = (summed * tissue).astype(BF16)
-            grad_out = gather(ut_ref).astype(F32) * (tissue * loss_factor)
             gs_ref[...] += fold(grad_out * branch)
-            grad_branch = (grad_out * scale).astype(BF16)
-            acc_ref[0] += mm_nt(active, grad_branch)
-            grad_active = mm(down_w, grad_branch)
-            grad_hidden = (grad_active * steepness).astype(BF16)
-            acc_ref[1] += mm_nt(grad_hidden, lowered)
-            grad_lowered = mm(up_w, grad_hidden)
             gg_ref[...] += fold(grad_lowered * normed)
             scaled = grad_lowered * gain
             mean_one = jnp.sum(scaled, axis=0, keepdims=True) * (1.0 / C)
             mean_two = jnp.sum(scaled * normed, axis=0, keepdims=True) * (1.0 / C)
             grad_mixed = (inverse * (scaled - mean_one - normed * mean_two)).astype(BF16)
-            for at, (w, j) in enumerate(columns):
+            for at, (w, j) in enumerate(pair_of(i)):
                 lanes = slice(LANES * at, LANES * (at + 1))
                 gm_ref[w, :, LANES * j : LANES * (j + 1)] = grad_mixed[:, lanes]
                 ft_ref[BLOCK * j + w] = features[:, lanes]
-            return carry
-
-        lax.fori_loop(0, BLOCK // 2, step, 0, unroll=STEP_UNROLL)
-
-    work((1, 2))
+
+        kept = []
+        state = front(0)
+        for i in range(BLOCK // 2):
+            pair = middle(state)
+            later = front(i + 1) if i + 1 < BLOCK // 2 else None
+            large(state, pair)
+            if defer:
+                kept.append((i, state, pair))
+            else:
+                back(i, state, pair)
+            state = later
+
+        def finish():
+            for i, state, pair in kept:
+                back(i, state, pair)
+
+        return finish
+
+    work((1, 2), False)
 
     for copy in sides_sent:
         copy.wait()
@@ -448,7 +499,7 @@
             both = side_ref[east * RIM + i]
             fill(east * (RIM + SIDE) + i, both[:, :LANES], both[:, LANES:])
 
-    work((0, 3))
+    finish = work((0, 3), True)
 
     def pieces(values):
         filled = jnp.concatenate([values, jnp.zeros((HID, 128 - C), F32)], axis=1)
@@ -463,6 +514,7 @@
             big_ref[half, i] = piece.astype(BF16)
     to_core = remote(big_ref.at[1 - core], core_in, sum_send.at[0], sum_recv.at[0], partner)
     to_core.start()
+    finish()
 
     def gradient(g):
         left = jnp.concatenate([gm_ref[w, GROUP * g : GROUP * (g + 1), :] for w in range(BLOCK)], axis=0)
@@ -538,29 +590,66 @@
 
     for w in range(0, SIDE, 4):
         part = jnp.concatenate([ft_ref[w + i] for i in range(4)], axis=0)
-        feat_ref[:, C * w : C * (w + 4)] = jnp.transpose(part)
+        feat_vmem[:, C * w : C * (w + 4)] = jnp.transpose(part)
+    store = pltpu.make_async_copy(feat_vmem, feat_ref, local_sem.at[10])
+    store.start()
 
     settle(small_y, 3, 5)
     total = small_y[0].astype(F32)
     for k in range(1, 4):
         total = total + small_y[k].astype(F32)
-    total = jnp.concatenate([total[:, :64], total[:, 64:]], axis=0)
-    total = jnp.transpose(jnp.concatenate([total, jnp.zeros((C, 64), F32)], axis=1))
-    out_dw_ref[...] = total[: KS * KS]
-    out_gain_ref[...] = total[KS * KS : KS * KS + 1]
-    out_scale_ref[...] = total[KS * KS + 1 : KS * KS + 2]
+    small_ref[...] = total
+    store_small = pltpu.make_async_copy(small_ref, small_out, local_sem.at[11])
+    store_small.start()
 
     settle(ag_buf.at[core], PLANE - 1, 6)
     last = remote(ag_buf.at[core], ag_buf.at[core], sum_send.at[7], sum_recv.at[7], partner)
     last.start()
     last.wait()
-    for half, ref in ((0, out_down_ref), (1, out_up_ref)):
-        joined = jnp.concatenate([ag_buf[half, i].astype(F32)[:PIECE] for i in range(PLANE)], axis=0)
+    store_sums = pltpu.make_async_copy(ag_buf, ag_out, local_sem.at[12])
+    store_sums.start()
+    for copy in (store, store_small, store_sums):
+        copy.wait()
+
+
+def finish_kernel(*refs):
+    inputs, outputs, refs = refs[:3], refs[3:9], refs[9:]
+    (feat, ag_ref, small_ref), refs = refs[:3], refs[3:]
+    (dw_ref, gain_ref, up_ref, down_ref, scale_ref), (sem_in, sem_out) = refs[:5], refs[5:]
+    coming = [
+        pltpu.make_async_copy(there, here, sem_in.at[i])
+        for i, (there, here) in enumerate(zip(inputs, (feat, ag_ref, small_ref)))
+    ]
+    results = (feat, dw_ref, gain_ref, up_ref, down_ref, scale_ref)
+    going = [
+        pltpu.make_async_copy(here, there, sem_out.at[i])
+        for i, (here, there) in enumerate(zip(results, outputs))
+    ]
+    for copy in coming:
+        copy.start()
+    coming[2].wait()
+    total = small_ref[...]
+    total = jnp.concatenate([total[:, :64], total[:, 64:]], axis=0)
+    total = jnp.transpose(jnp.concatenate([total, jnp.zeros((C, 64), F32)], axis=1))
+    dw_ref[...] = total[: KS * KS]
+    gain_ref[...] = total[KS * KS : KS * KS + 1]
+    scale_ref[...] = total[KS * KS + 1 : KS * KS + 2]
+    for i in (1, 2, 5):
+        going[i].start()
+    coming[1].wait()
+    for half, ref in ((0, down_ref), (1, up_ref)):
+        joined = jnp.concatenate([ag_ref[half, i].astype(F32)[:PIECE] for i in range(PLANE)], axis=0)
         ref[...] = jnp.transpose(joined)[:C]
-
-
-def vmem(count):
-    return [pl.BlockSpec(memory_space=pltpu.VMEM)] * count
+    for i in (3, 4):
+        going[i].start()
+    coming[0].wait()
+    going[0].start()
+    for copy in going:
+        copy.wait()
+
+
+def anywhere(count):
+    return [pl.BlockSpec(memory_space=pl.ANY)] * count
 
 
 def local(
@@ -579,22 +668,36 @@
     tiles = lax.axis_size("tile")
     loss_factor = (tiles * lax.axis_size("slab") * SLOTS * SIDE * SIDE) ** (-0.5)
     dma = pltpu.SemaphoreType.DMA
-    features, grad_dw, grad_gain, grad_up, grad_down_t, grad_scale = pl.pallas_call(
+    operands = (
+        pixels[0],
+        stem_weight,
+        stem_gain[None],
+        upstream.reshape(LANES, SIDE * C),
+        tissue[0],
+        dw_weight,
+        norm_gain[None],
+        up_weight,
+        down_weight.T,
+        layer_scale[None],
+    )
+    features, gathered, small = pl.pallas_call(
         functools.partial(whole_kernel, tiles, loss_factor),
         out_shape=(
             jax.ShapeDtypeStruct((LANES, SIDE * C), BF16),
-            jax.ShapeDtypeStruct((KS * KS, C), F32),
-            jax.ShapeDtypeStruct((1, C), F32),
-            jax.ShapeDtypeStruct((C, HID), F32),
-            jax.ShapeDtypeStruct((C, HID), F32),
-            jax.ShapeDtypeStruct((1, C), F32),
+            jax.ShapeDtypeStruct((2, PLANE, PIECE_PAD, 128), BF16),
+            jax.ShapeDtypeStruct((C // 2, 128), F32),
         ),
-        in_specs=[pl.BlockSpec(memory_space=pltpu.SMEM)] + vmem(10),
-        out_specs=tuple(vmem(6)),
-        scratch_shapes=[
+        in_specs=[pl.BlockSpec(memory_space=pltpu.SMEM)] + anywhere(10),
+        out_specs=tuple(anywhere(3)),
+        scratch_shapes=[pltpu.VMEM(x.shape, x.dtype) for x in operands]
+        + [
+            pltpu.VMEM((LANES, SIDE * C), BF16),
+            pltpu.VMEM((2, PLANE, PIECE_PAD, 128), BF16),
+            pltpu.VMEM((C // 2, 128), F32),
             pltpu.VMEM((SIDE, C, LANES), BF16),
-            pltpu.VMEM((2 * RIM, C, LANES), BF16),
-            pltpu.VMEM((2 * REACH + 2, RIM, C, LANES), BF16),
+            pltpu.VMEM((2, C, LANES), BF16),
+            pltpu.VMEM((2, C, LANES), BF16),
+            pltpu.VMEM((2 * REACH, RIM, C, LANES), BF16),
             pltpu.VMEM((KS, PADW, C, LANES), BF16),
             pltpu.VMEM((SIDE, C, LANES), BF16),
             pltpu.VMEM((2 * RIM, C, 2 * LANES), BF16),
@@ -612,7 +715,6 @@
             pltpu.VMEM((PLANE, PIECE_PAD, 128), BF16),
             pltpu.VMEM((PLANE, PIECE_PAD, 128), BF16),
             pltpu.VMEM((4, PIECE_PAD, 128), BF16),
-            pltpu.VMEM((2, PLANE, PIECE_PAD, 128), BF16),
             pltpu.VMEM((2, C // 2, 128), BF16),
             pltpu.VMEM((PLANE, C // 2, 128), BF16),
             pltpu.VMEM((4, C // 2, 128), BF16),
@@ -620,24 +722,40 @@
             dma((2 * REACH + 2,)),
             dma((8,)),
             dma((8,)),
+            dma((13,)),
         ],
         compiler_params=pltpu.CompilerParams(
-            collective_id=0, has_side_effects=True, vmem_limit_bytes=56 * 1024 * 1024
+            collective_id=0, has_side_effects=True, vmem_limit_bytes=VMEM_BYTES
         ),
         name="whole",
-    )(
-        neighbours[0],
-        pixels[0],
-        stem_weight,
-        stem_gain[None],
-        upstream.reshape(LANES, SIDE * C),
-        tissue[0],
-        dw_weight,
-        norm_gain[None],
-        up_weight,
-        down_weight.T,
-        layer_scale[None],
-    )
+    )(neighbours[0], *operands)
+    features, grad_dw, grad_gain, grad_up, grad_down_t, grad_scale = pl.pallas_call(
+        finish_kernel,
+        out_shape=(
+            jax.ShapeDtypeStruct((LANES, SIDE * C), BF16),
+            jax.ShapeDtypeStruct((KS * KS, C), F32),
+            jax.ShapeDtypeStruct((1, C), F32),
+            jax.ShapeDtypeStruct((C, HID), F32),
+            jax.ShapeDtypeStruct((C, HID), F32),
+            jax.ShapeDtypeStruct((1, C), F32),
+        ),
+        in_specs=anywhere(3),
+        out_specs=tuple(anywhere(6)),
+        scratch_shapes=[
+            pltpu.VMEM((LANES, SIDE * C), BF16),
+            pltpu.VMEM((2, PLANE, PIECE_PAD, 128), BF16),
+            pltpu.VMEM((C // 2, 128), F32),
+            pltpu.VMEM((KS * KS, C), F32),
+            pltpu.VMEM((1, C), F32),
+            pltpu.VMEM((C, HID), F32),
+            pltpu.VMEM((C, HID), F32),
+            pltpu.VMEM((1, C), F32),
+            dma((3,)),
+            dma((6,)),
+        ],
+        compiler_params=pltpu.CompilerParams(vmem_limit_bytes=VMEM_BYTES),
+        name="finish",
+    )(features, gathered, small)
     return (
         features.reshape(upstream.shape),
         grad_dw,

time: 53.1 us -> 47.7 us (0.90)
  local copies, waits for them, and re-layouts: 5.39 us -> 0 us
    unnamed x16 -> x0, local copies, waits for them, and re-layouts: 5.39 us -> none
    pallas_call x1, Pallas kernels: 46.8 us -> 44.3 us  [local(): pl.pallas_call(functools.partial(whole_kernel, tiles, loss_factor), out_s...]
    pallas_call x0 -> x1, Pallas kernels: none -> 2.4 us  [local(): pl.pallas_call(finish_kernel, out_shape=(jax.ShapeDtypeStruct((LANES, SID...]
where the time goes in v2:
time: 47.7 us; the launch traced here: 47.5 us
  Pallas kernels  46.7 us (98%)
  between operations  0.8 us (2%)
    pallas_call x1, Pallas kernels, local(): pl.pallas_call(functools.partial(whole_kernel, tiles, loss_factor), out_s...  44.3 us
    pallas_call x1, Pallas kernels, local(): pl.pallas_call(finish_kernel, out_shape=(jax.ShapeDtypeStruct((LANES, SID...  2.4 us

profile of v2, /device:TPU:1, one launch (start us, length us, event | category | flops | bytes accessed | tf_op | source)
XLA Modules:
  0.0 47.5 jit_solution(15263614563788570415)
XLA Ops:
  0.6 44.3 %whole.1 = (bf16[128,3072]{1,0:T(8,128)(2,1)}, bf16[2,16,32,128]{3,2,1,0:T(8,128)(2,1)}, f32[48,128]{1,0:T(8,128)}) custom-call(s32[4,8]{1,0:T(4,128)} %bitcast.16, bf16[4,128,384]{2,1,0:T(8,128)(2,1)} %bitcast.13, bf16[48,96]{1,0:T(8,128)(2,1)} %refs_1_.1, f32[1,96]{1,0:T(1,128)} %bitcast.17, bf16[128,3072]{1,0:T(8,128)(2,1)} %bitcast.12, ...), custom_call_target="tpu_custom_call" | custom-call | tf_op jit(solution)/shard_map/whole/pallas_call | solution.py:683
  45.0 2.4 %finish.1 = (bf16[128,3072]{1,0:T(8,128)(2,1)}, f32[49,96]{1,0:T(8,128)}, f32[1,96]{1,0:T(1,128)}, f32[96,384]{1,0:T(8,128)}, f32[96,384]{1,0:T(8,128)}, /*index=5*/f32[1,96]{1,0:T(1,128)}) custom-call(bf16[128,3072]{1,0:T(8,128)(2,1)} %get-tuple-element.15.refs_0_, bf16[2,16,32,128]{3,2,1,0:T(8,128)(2,1)} %get-tuple-element.16.refs_1_, ...), custom_call_target="tpu_custom_call" | custom-call | tf_op jit(solution)/shard_map/finish/pallas_call | solution.py:732

commit v3 on v2

--- a/solution.py
+++ b/solution.py
@@ -118,7 +118,7 @@
         rs_src,
         rs_in,
         y_buf,
-        small_core,
+        dw_part,
         small_plane,
         small_y,
         send_sem,
@@ -147,18 +147,19 @@
         i = lax.rem(me_plane + k, PLANE)
         return i, {"tile": y_lo * PLANE + i, "slab": slab}
 
-    def y_peer(k):
+    def y_peer(k, at=core):
         other_lo = lax.rem(y_lo + k % 2, 2)
         other_hi = lax.rem(y_hi + k // 2, 2)
-        return {"tile": other_lo * PLANE + me_plane, "slab": 2 * other_hi + core}
+        return {"tile": other_lo * PLANE + me_plane, "slab": 2 * other_hi + at}
+
+    column_peers = [y_peer(k) for k in range(1, 4)] + [y_peer(k, 1 - core) for k in range(4)]
 
     barrier = pltpu.get_barrier_semaphore()
     greeted = [
         {"tile": lax.rem(me + sign * d + tiles, tiles)} for d in range(1, REACH + 1) for sign in (-1, 1)
     ]
-    greeted += [partner]
     greeted += [plane_peer(k)[1] for k in range(1, PLANE)]
-    greeted += [y_peer(k) for k in range(1, 4)]
+    greeted += column_peers
     for device in greeted:
         pl.semaphore_signal(barrier, inc=1, device_id=device, device_id_type=MESH)
 
@@ -234,6 +235,10 @@
         if d == 1:
             strips_sent.append((strip_ref.at[0], strip_in.at[0], 10, back))
             strips_sent.append((strip_ref.at[1], strip_in.at[1], 11, ahead))
+        if d == REACH:
+            sides_sent.append((strip_ref.at[0], strip_in.at[2], d - 1, back))
+            sides_sent.append((strip_ref.at[1], strip_in.at[3], REACH + d - 1, ahead))
+            continue
         sides_sent.append((ct_ref.at[pl.ds(0, RIM)], recv_ref.at[d - 1], d - 1, back))
         at = REACH + d - 1
         sides_sent.append((ct_ref.at[pl.ds(SIDE - RIM, RIM)], recv_ref.at[at], at, ahead))
@@ -457,13 +462,36 @@
                 back(i, state, pair)
             state = later
 
-        def finish():
-            for i, state, pair in kept:
-                back(i, state, pair)
+        def finish(some):
+            for i in some:
+                back(*kept[i])
 
         return finish
 
     work((1, 2), False)
+
+    def gradient(g, blocks):
+        left = jnp.concatenate(
+            [
+                jnp.concatenate(
+                    [gm_ref[w, GROUP * g : GROUP * (g + 1), LANES * j : LANES * (j + 1)] for j in blocks],
+                    axis=1,
+                )
+                for w in range(BLOCK)
+            ],
+            axis=0,
+        )
+        full = mm_nt(left, window(g, blocks))
+        total = None
+        for w in range(BLOCK):
+            part = jnp.where(diagonal, full[GROUP * w : GROUP * (w + 1)], 0.0)
+            if w:
+                part = pltpu.roll(part, BAND - GROUP * w, 1)
+            total = part if total is None else total + part
+        return total
+
+    for g in range(GROUPS):
+        dw_part[g] = gradient(g, (1, 2))
 
     for copy in sides_sent:
         copy.wait()
@@ -477,14 +505,19 @@
         above = spread(per_tile(4 + east, rule), -1)
         below = spread(per_tile(6 + east, rule), 1)
         halo = jnp.where(top, above, jnp.where(bottom, below, -1))
-        index = jnp.concatenate([add_row(straight, row_of), add_row(halo, row_of)], axis=1)
+        corner = REACH * LANES + SIDE * jnp.where(top, row_of - (SIDE - RIM), row_of)
+        halo = jnp.where(halo >= REACH * LANES, corner, add_row(halo, row_of))
+        index = jnp.concatenate([add_row(straight, row_of), halo], axis=1)
         select = onehot(iota(((REACH + 1) * LANES, 2 * LANES), 0) == index)
         first = 0 if east else SIDE - RIM
         base = 0 if east else REACH
         source = jnp.concatenate(
             [
                 jnp.concatenate(
-                    [ct_ref[first + i]] + [recv_ref[base + d, i] for d in range(REACH)], axis=1
+                    [ct_ref[first + i]]
+                    + [recv_ref[base + d, i] for d in range(REACH - 1)]
+                    + [pltpu.roll(strip_in[3 - east], (LANES - first - i) % LANES, 1)],
+                    axis=1,
                 )
                 for i in range(RIM)
             ],
@@ -501,37 +534,18 @@
 
     finish = work((0, 3), True)
 
-    def pieces(values):
-        filled = jnp.concatenate([values, jnp.zeros((HID, 128 - C), F32)], axis=1)
-        out = []
-        for i in range(PLANE):
-            piece = filled[PIECE * i : PIECE * (i + 1)]
-            out.append(jnp.concatenate([piece, jnp.zeros((PIECE_PAD - PIECE, 128), F32)], axis=0))
-        return out
-
-    for half in range(2):
-        for i, piece in enumerate(pieces(acc_ref[half])):
-            big_ref[half, i] = piece.astype(BF16)
-    to_core = remote(big_ref.at[1 - core], core_in, sum_send.at[0], sum_recv.at[0], partner)
+    lane_pad = jnp.zeros((HID, 128 - C), F32)
+    row_pad = jnp.zeros((PIECE_PAD - PIECE, 128), F32)
+    big_ref[...] = jnp.concatenate([acc_ref[1 - core], lane_pad], axis=1).astype(BF16)
+    to_core = remote(big_ref, core_in, sum_send.at[0], sum_recv.at[0], partner)
     to_core.start()
-    finish()
-
-    def gradient(g):
-        left = jnp.concatenate([gm_ref[w, GROUP * g : GROUP * (g + 1), :] for w in range(BLOCK)], axis=0)
-        full = mm_nt(left, window(g, range(BLOCKS)))
-        total = None
-        for w in range(BLOCK):
-            part = jnp.where(diagonal, full[GROUP * w : GROUP * (w + 1)], 0.0)
-            if w:
-                part = pltpu.roll(part, BAND - GROUP * w, 1)
-            total = part if total is None else total + part
-        return total
-
-    totals = [gradient(g) for g in range(GROUPS // 2)]
+    finish(range(1))
 
     to_core.wait()
+    both = jnp.concatenate([acc_ref[core], lane_pad], axis=1) + core_in[...].astype(F32)
     for i in range(PLANE):
-        rs_src[i] = (big_ref[core, i].astype(F32) + core_in[i].astype(F32)).astype(BF16)
+        piece = jnp.concatenate([both[PIECE * i : PIECE * (i + 1)], row_pad], axis=0)
+        rs_src[i] = piece.astype(BF16)
 
     def scatter(target, source, at):
         for k in range(1, PLANE):
@@ -544,8 +558,9 @@
         copy.wait()
 
     scatter(lambda k: rs_in.at[k], lambda i: rs_src.at[i], 1)
-
-    totals += [gradient(g) for g in range(GROUPS // 2, GROUPS)]
+    finish(range(1, 4))
+
+    totals = [dw_part[g] + gradient(g, (0, 3)) for g in range(GROUPS)]
     totals = jnp.concatenate(totals, axis=0).astype(BF16)
     k_at, n_at = iota((BAND, LANES), 0), iota((BAND, LANES), 1)
     col_at = (k_at % TAPW) // GROUP
@@ -555,13 +570,6 @@
     small = jnp.where(n_at == KS * KS, jnp.sum(gg_ref[...], axis=1, keepdims=True), small)
     small = jnp.where(n_at == KS * KS + 1, jnp.sum(gs_ref[...], axis=1, keepdims=True), small)
     small = jnp.concatenate([small[: C // 2, :64], small[C // 2 :, :64]], axis=1).astype(BF16)
-    small_core[core] = small
-    small_to_core = remote(
-        small_core.at[core], small_core.at[core], sum_send.at[2], sum_recv.at[2], partner
-    )
-    small_to_core.start()
-    small_to_core.wait()
-    small = (small_core[0].astype(F32) + small_core[1].astype(F32)).astype(BF16)
     small_plane[me_plane] = small
     scatter(lambda k: small_plane.at[me_plane], lambda i: small_plane.at[me_plane], 3)
 
@@ -577,9 +585,10 @@
     total = small_plane[0].astype(F32)
     for k in range(1, PLANE):
         total = total + small_plane[k].astype(F32)
-    small_y[me_y] = total.astype(BF16)
-    for k in range(1, 4):
-        remote(small_y.at[me_y], small_y.at[me_y], sum_send.at[5], sum_recv.at[5], y_peer(k)).start()
+    at = 4 * core + me_y
+    small_y[at] = total.astype(BF16)
+    for device in column_peers:
+        remote(small_y.at[at], small_y.at[at], sum_send.at[5], sum_recv.at[5], device).start()
 
     settle(y_buf, 3, 4)
     total = y_buf[0].astype(F32)
@@ -594,9 +603,9 @@
     store = pltpu.make_async_copy(feat_vmem, feat_ref, local_sem.at[10])
     store.start()
 
-    settle(small_y, 3, 5)
+    settle(small_y, 7, 5)
     total = small_y[0].astype(F32)
-    for k in range(1, 4):
+    for k in range(1, 8):
         total = total + small_y[k].astype(F32)
     small_ref[...] = total
     store_small = pltpu.make_async_copy(small_ref, small_out, local_sem.at[11])
@@ -696,7 +705,7 @@
             pltpu.VMEM((C // 2, 128), F32),
             pltpu.VMEM((SIDE, C, LANES), BF16),
             pltpu.VMEM((2, C, LANES), BF16),
-            pltpu.VMEM((2, C, LANES), BF16),
+            pltpu.VMEM((4, C, LANES), BF16),
             pltpu.VMEM((2 * REACH, RIM, C, LANES), BF16),
             pltpu.VMEM((KS, PADW, C, LANES), BF16),
             pltpu.VMEM((SIDE, C, LANES), BF16),
@@ -710,14 +719,14 @@
             pltpu.VMEM((2, HID, C), F32),
             pltpu.VMEM((C, LANES), F32),
             pltpu.VMEM((C, LANES), F32),
-            pltpu.VMEM((2, PLANE, PIECE_PAD, 128), BF16),
-            pltpu.VMEM((PLANE, PIECE_PAD, 128), BF16),
+            pltpu.VMEM((HID, 128), BF16),
+            pltpu.VMEM((HID, 128), BF16),
             pltpu.VMEM((PLANE, PIECE_PAD, 128), BF16),
             pltpu.VMEM((PLANE, PIECE_PAD, 128), BF16),
             pltpu.VMEM((4, PIECE_PAD, 128), BF16),
-            pltpu.VMEM((2, C // 2, 128), BF16),
+            pltpu.VMEM((GROUPS, GROUP, BAND), F32),
             pltpu.VMEM((PLANE, C // 2, 128), BF16),
-            pltpu.VMEM((4, C // 2, 128), BF16),
+            pltpu.VMEM((8, C // 2, 128), BF16),
             dma((2 * REACH + 2,)),
             dma((2 * REACH + 2,)),
             dma((8,)),

time: 47.7 us -> 46.7 us (0.979)
  Pallas kernels: 46.7 us -> 45.7 us
    pallas_call x1, Pallas kernels: 44.3 us -> 43.3 us  [local(): pl.pallas_call(functools.partial(whole_kernel, tiles, loss_factor), out_s...]
where the time goes in v3:
time: 46.7 us; the launch traced here: 46.5 us
  Pallas kernels  45.7 us (98%)
  between operations  0.8 us (2%)
    pallas_call x1, Pallas kernels, local(): pl.pallas_call(functools.partial(whole_kernel, tiles, loss_factor), out_s...  43.3 us
    pallas_call x1, Pallas kernels, local(): pl.pallas_call(finish_kernel, out_shape=(jax.ShapeDtypeStruct((LANES, SID...  2.4 us

profile of v3, /device:TPU:1, one launch (start us, length us, event | category | flops | bytes accessed | tf_op | source)
XLA Modules:
  0.0 46.5 jit_solution(6498191307566949356)
XLA Ops:
  0.6 43.3 %whole.1 = (bf16[128,3072]{1,0:T(8,128)(2,1)}, bf16[2,16,32,128]{3,2,1,0:T(8,128)(2,1)}, f32[48,128]{1,0:T(8,128)}) custom-call(s32[4,8]{1,0:T(4,128)} %bitcast.16, bf16[4,128,384]{2,1,0:T(8,128)(2,1)} %bitcast.13, bf16[48,96]{1,0:T(8,128)(2,1)} %refs_1_.1, f32[1,96]{1,0:T(1,128)} %bitcast.17, bf16[128,3072]{1,0:T(8,128)(2,1)} %bitcast.12, ...), custom_call_target="tpu_custom_call" | custom-call | tf_op jit(solution)/shard_map/whole/pallas_call | solution.py:692
  44.0 2.4 %finish.1 = (bf16[128,3072]{1,0:T(8,128)(2,1)}, f32[49,96]{1,0:T(8,128)}, f32[1,96]{1,0:T(1,128)}, f32[96,384]{1,0:T(8,128)}, f32[96,384]{1,0:T(8,128)}, /*index=5*/f32[1,96]{1,0:T(1,128)}) custom-call(bf16[128,3072]{1,0:T(8,128)(2,1)} %get-tuple-element.15.refs_0_, bf16[2,16,32,128]{3,2,1,0:T(8,128)(2,1)} %get-tuple-element.16.refs_1_, ...), custom_call_target="tpu_custom_call" | custom-call | tf_op jit(solution)/shard_map/finish/pallas_call | solution.py:741

commit v4 on v3

--- a/solution.py
+++ b/solution.py
@@ -20,7 +20,7 @@
 PADW = SIDE + 2 * RIM
 GROUP = 16
 GROUPS = C // GROUP
-BLOCK = 8
+BLOCK = 4
 BLOCKS = SIDE // BLOCK
 TAPW = (BLOCK + RIM * 2) * GROUP
 BAND = KS * TAPW
@@ -118,13 +118,13 @@
         rs_src,
         rs_in,
         y_buf,
-        dw_part,
         small_plane,
         small_y,
         send_sem,
         recv_sem,
         sum_send,
         sum_recv,
+        gather_recv,
         local_sem,
     ) = refs
     me = lax.axis_index("tile")
@@ -400,10 +400,13 @@
         for g in range(GROUPS):
             out = mm(band_ref[g], window(g, blocks))
             for w in range(BLOCK):
-                mixed_ref[w, GROUP * g : GROUP * (g + 1), :] = out[GROUP * w : GROUP * (w + 1)]
+                mixed_ref[w, GROUP * g : GROUP * (g + 1), : out.shape[1]] = out[GROUP * w : GROUP * (w + 1)]
+
+        columns = [(w, j) for w in range(BLOCK) for j in blocks]
+        steps = len(columns) // 4
 
         def pair_of(i):
-            return [(2 * i + v, j) for v in range(2) for j in blocks]
+            return columns[4 * i : 4 * (i + 1)]
 
         def gather(ref, i):
             return jnp.concatenate([ref[BLOCK * j + w] for w, j in pair_of(i)], axis=1)
@@ -413,7 +416,8 @@
             grad_out = gather(ut_ref, i).astype(F32) * (tissue * loss_factor)
             grad_branch = (grad_out * scale).astype(BF16)
             grad_active = mm(down_w, grad_branch)
-            mixed = jnp.concatenate([mixed_ref[2 * i], mixed_ref[2 * i + 1]], axis=1)
+            places = [(w, LANES * blocks.index(j)) for w, j in pair_of(i)]
+            mixed = jnp.concatenate([mixed_ref[w, :, at : at + LANES] for w, at in places], axis=1)
             mean = jnp.sum(mixed, axis=0, keepdims=True) * (1.0 / C)
             centered = mixed - mean
             inverse = lax.rsqrt(jnp.sum(centered * centered, axis=0, keepdims=True) * (1.0 / C) + EPS)
@@ -452,9 +456,9 @@
 
         kept = []
         state = front(0)
-        for i in range(BLOCK // 2):
+        for i in range(steps):
             pair = middle(state)
-            later = front(i + 1) if i + 1 < BLOCK // 2 else None
+            later = front(i + 1) if i + 1 < steps else None
             large(state, pair)
             if defer:
                 kept.append((i, state, pair))
@@ -468,7 +472,7 @@
 
         return finish
 
-    work((1, 2), False)
+    work(tuple(range(1, BLOCKS - 1)), False)
 
     def gradient(g, blocks):
         left = jnp.concatenate(
@@ -490,8 +494,6 @@
             total = part if total is None else total + part
         return total
 
-    for g in range(GROUPS):
-        dw_part[g] = gradient(g, (1, 2))
 
     for copy in sides_sent:
         copy.wait()
@@ -532,7 +534,7 @@
             both = side_ref[east * RIM + i]
             fill(east * (RIM + SIDE) + i, both[:, :LANES], both[:, LANES:])
 
-    finish = work((0, 3), True)
+    finish = work((0, BLOCKS - 1), True)
 
     lane_pad = jnp.zeros((HID, 128 - C), F32)
     row_pad = jnp.zeros((PIECE_PAD - PIECE, 128), F32)
@@ -558,9 +560,9 @@
         copy.wait()
 
     scatter(lambda k: rs_in.at[k], lambda i: rs_src.at[i], 1)
-    finish(range(1, 4))
-
-    totals = [dw_part[g] + gradient(g, (0, 3)) for g in range(GROUPS)]
+    finish(range(1, 2))
+
+    totals = [gradient(g, range(BLOCKS)) for g in range(GROUPS)]
     totals = jnp.concatenate(totals, axis=0).astype(BF16)
     k_at, n_at = iota((BAND, LANES), 0), iota((BAND, LANES), 1)
     col_at = (k_at % TAPW) // GROUP
@@ -595,7 +597,10 @@
     for k in range(1, 4):
         total = total + y_buf[k].astype(F32)
     ag_buf[core, me_plane] = total.astype(BF16)
-    scatter(lambda k: ag_buf.at[core, me_plane], lambda i: ag_buf.at[core, me_plane], 6)
+    mine = ag_buf.at[core, me_plane]
+    for k in range(1, PLANE):
+        remote(mine, mine, sum_send.at[6], gather_recv.at[k], plane_peer(k)[1]).start()
+    remote(mine, mine, sum_send.at[7], sum_recv.at[7], partner).start()
 
     for w in range(0, SIDE, 4):
         part = jnp.concatenate([ft_ref[w + i] for i in range(4)], axis=0)
@@ -611,10 +616,14 @@
     store_small = pltpu.make_async_copy(small_ref, small_out, local_sem.at[11])
     store_small.start()
 
-    settle(ag_buf.at[core], PLANE - 1, 6)
-    last = remote(ag_buf.at[core], ag_buf.at[core], sum_send.at[7], sum_recv.at[7], partner)
-    last.start()
-    last.wait()
+    for k in range(1, PLANE):
+        piece = ag_buf.at[core, lax.rem(me_plane + PLANE - k, PLANE)]
+        remote(piece, piece, sum_send.at[6], gather_recv.at[k], partner).wait_recv()
+        remote(piece, piece, sum_send.at[7], sum_recv.at[7], partner).start()
+    sent = ag_buf.at[core, pl.ds(0, PLANE - 1)]
+    remote(sent, sent, sum_send.at[6], sum_recv.at[6], partner).wait_send()
+    other = ag_buf.at[1 - core]
+    remote(other, other, sum_send.at[7], sum_recv.at[7], partner).wait()
     store_sums = pltpu.make_async_copy(ag_buf, ag_out, local_sem.at[12])
     store_sums.start()
     for copy in (store, store_small, store_sums):
@@ -636,6 +645,8 @@
     ]
     for copy in coming:
         copy.start()
+    coming[0].wait()
+    going[0].start()
     coming[2].wait()
     total = small_ref[...]
     total = jnp.concatenate([total[:, :64], total[:, 64:]], axis=0)
@@ -651,8 +662,6 @@
         ref[...] = jnp.transpose(joined)[:C]
     for i in (3, 4):
         going[i].start()
-    coming[0].wait()
-    going[0].start()
     for copy in going:
         copy.wait()
 
@@ -711,7 +720,7 @@
             pltpu.VMEM((SIDE, C, LANES), BF16),
             pltpu.VMEM((2 * RIM, C, 2 * LANES), BF16),
             pltpu.VMEM((GROUPS, BLOCK * GROUP, BAND), BF16),
-            pltpu.VMEM((BLOCK, C, 2 * LANES), F32),
+            pltpu.VMEM((BLOCK, C, (BLOCKS - 2) * LANES), F32),
             pltpu.VMEM((BLOCK, C, BLOCKS * LANES), BF16),
             pltpu.VMEM((SIDE, C, LANES), BF16),
             pltpu.VMEM((SIDE, C, LANES), BF16),
@@ -724,13 +733,13 @@
             pltpu.VMEM((PLANE, PIECE_PAD, 128), BF16),
             pltpu.VMEM((PLANE, PIECE_PAD, 128), BF16),
             pltpu.VMEM((4, PIECE_PAD, 128), BF16),
-            pltpu.VMEM((GROUPS, GROUP, BAND), F32),
             pltpu.VMEM((PLANE, C // 2, 128), BF16),
             pltpu.VMEM((8, C // 2, 128), BF16),
             dma((2 * REACH + 2,)),
             dma((2 * REACH + 2,)),
             dma((8,)),
             dma((8,)),
+            dma((PLANE,)),
             dma((13,)),
         ],
         compiler_params=pltpu.CompilerParams(

time: 46.7 us -> 46.2 us (0.989)
  Pallas kernels: 45.7 us -> 45.2 us
where the time goes in v4:
time: 46.2 us; the launch traced here: 46 us
  Pallas kernels  45.2 us (98%)
  between operations  0.8 us (2%)
    pallas_call x1, Pallas kernels, local(): pl.pallas_call(functools.partial(whole_kernel, tiles, loss_factor), out_s...  43 us
    pallas_call x1, Pallas kernels, local(): pl.pallas_call(finish_kernel, out_shape=(jax.ShapeDtypeStruct((LANES, SID...  2.2 us

profile of v4, /device:TPU:1, one launch (start us, length us, event | category | flops | bytes accessed | tf_op | source)
XLA Modules:
  0.0 46.0 jit_solution(18366905166769172245)
XLA Ops:
  0.6 43.0 %whole.1 = (bf16[128,3072]{1,0:T(8,128)(2,1)}, bf16[2,16,32,128]{3,2,1,0:T(8,128)(2,1)}, f32[48,128]{1,0:T(8,128)}) custom-call(s32[4,8]{1,0:T(4,128)} %bitcast.16, bf16[4,128,384]{2,1,0:T(8,128)(2,1)} %bitcast.13, bf16[48,96]{1,0:T(8,128)(2,1)} %refs_1_.1, f32[1,96]{1,0:T(1,128)} %bitcast.17, bf16[128,3072]{1,0:T(8,128)(2,1)} %bitcast.12, ...), custom_call_target="tpu_custom_call" | custom-call | tf_op jit(solution)/shard_map/whole/pallas_call | solution.py:701
  43.6 2.2 %finish.1 = (bf16[128,3072]{1,0:T(8,128)(2,1)}, f32[49,96]{1,0:T(8,128)}, f32[1,96]{1,0:T(1,128)}, f32[96,384]{1,0:T(8,128)}, f32[96,384]{1,0:T(8,128)}, /*index=5*/f32[1,96]{1,0:T(1,128)}) custom-call(bf16[128,3072]{1,0:T(8,128)(2,1)} %get-tuple-element.15.refs_0_, bf16[2,16,32,128]{3,2,1,0:T(8,128)(2,1)} %get-tuple-element.16.refs_1_, ...), custom_call_target="tpu_custom_call" | custom-call | tf_op jit(solution)/shard_map/finish/pallas_call | solution.py:750

commit v5 on v4

--- a/solution.py
+++ b/solution.py
@@ -252,7 +252,7 @@
         return started
 
     strips_sent = launch(strips_sent)
-    sides_sent = launch(sides_sent)
+    sides_sent = launch([sides_sent[i] for i in (0, 1, 6, 7, 4, 5, 2, 3, 8, 9)])
 
     for copy in fetches[3:]:
         copy.wait()

time: 46.2 us -> 46.1 us (level)
  no operation moved by 1% of the time
where the time goes in v5:
time: 46.1 us; the launch traced here: 46 us
  Pallas kernels  45.2 us (98%)
  between operations  0.8 us (2%)
    pallas_call x1, Pallas kernels, local(): pl.pallas_call(functools.partial(whole_kernel, tiles, loss_factor), out_s...  43 us
    pallas_call x1, Pallas kernels, local(): pl.pallas_call(finish_kernel, out_shape=(jax.ShapeDtypeStruct((LANES, SID...  2.2 us

profile of v5, /device:TPU:1, one launch (start us, length us, event | category | flops | bytes accessed | tf_op | source)
XLA Modules:
  0.0 46.0 jit_solution(436852809002912581)
XLA Ops:
  0.6 43.0 %whole.1 = (bf16[128,3072]{1,0:T(8,128)(2,1)}, bf16[2,16,32,128]{3,2,1,0:T(8,128)(2,1)}, f32[48,128]{1,0:T(8,128)}) custom-call(s32[4,8]{1,0:T(4,128)} %bitcast.16, bf16[4,128,384]{2,1,0:T(8,128)(2,1)} %bitcast.13, bf16[48,96]{1,0:T(8,128)(2,1)} %refs_1_.1, f32[1,96]{1,0:T(1,128)} %bitcast.17, bf16[128,3072]{1,0:T(8,128)(2,1)} %bitcast.12, ...), custom_call_target="tpu_custom_call" | custom-call | tf_op jit(solution)/shard_map/whole/pallas_call | solution.py:701
  43.6 2.2 %finish.1 = (bf16[128,3072]{1,0:T(8,128)(2,1)}, f32[49,96]{1,0:T(8,128)}, f32[1,96]{1,0:T(1,128)}, f32[96,384]{1,0:T(8,128)}, f32[96,384]{1,0:T(8,128)}, /*index=5*/f32[1,96]{1,0:T(1,128)}) custom-call(bf16[128,3072]{1,0:T(8,128)(2,1)} %get-tuple-element.15.refs_0_, bf16[2,16,32,128]{3,2,1,0:T(8,128)(2,1)} %get-tuple-element.16.refs_1_, ...), custom_call_target="tpu_custom_call" | custom-call | tf_op jit(solution)/shard_map/finish/pallas_call | solution.py:750
